TPU v7x, 1024 devices: a whole 4x4x32 slice. The times are simulated.
1024 devices in a mesh: seq: 128 (over x, z), tp: 4 (over y), dp: 2 (over core).
Axes of the slice: x: 4, y: 4, z: 32, core: 2. Of those that a mesh axis runs over, the one named last changes fastest.
Arguments:
- frames: bfloat16 [65536, 1536], P(('seq', 'dp')), may hold values from -6 to 6
- lengths: int32 [4], replicated, may hold values from 1 to 32768, 65536 in all
- norm_gain: float32 [1536], replicated, may hold values from 0.25 to 1.75
- qkv_weight: bfloat16 [1536, 3, 1536], P(None, None, 'tp'), may hold values from -0.15625 to 0.15625
- out_weight: bfloat16 [1536, 1536], P('tp'), may hold values from -0.15625 to 0.15625
- conv_gain: float32 [1536], replicated, may hold values from 0.25 to 1.75
- glu_weight: bfloat16 [1536, 2, 1536], P(None, None, 'tp'), may hold values from -0.15625 to 0.15625
- conv_taps: float32 [31, 1536], P(None, 'tp'), may hold values from -1 to 1
- point_weight: bfloat16 [1536, 1536], P('tp'), may hold values from -0.15625 to 0.15625
Outputs:
- layer_out: bfloat16 [65536, 1536], P(('seq', 'dp'), 'tp')
Inputs may be any that keep to these rules, and one draw needn't show every extreme that they name: The lengths of the utterances packed in order into the stream; they sum to 65536 and the longest is exactly 32768.
All inputs are finite; a program needn't handle non-finite values.
Results may differ from a plain program's by a relative error of at most 0.012.
Values may be sent and summed in bfloat16 or wider, within the bound.
No kernel may reach another device: no remote copies, remote signals or barrier semaphores. Data moves between devices by JAX's collectives and lax.ppermute only.
A program may use at most 64 MiB of HBM per device.

v0:
```python
import jax
import jax.numpy as jnp
from jax import lax
from jax.sharding import PartitionSpec as P

HEAD = 96
KERNEL = 31


EPSILON = 1e-05


def padded_2(x, sides, width):
    for axis, dim in sides:
        devices, length = (lax.axis_size(axis), x.shape[dim])
        up = [(i, (i + 1) % devices) for i in range(devices - 1)]
        down = [(j, i) for i, j in up]
        last = lax.slice_in_dim(x, length - width, length, axis=dim)
        initial = lax.slice_in_dim(x, 0, width, axis=dim)
        before = lax.ppermute(last, axis, up)
        after = lax.ppermute(initial, axis, down)
        x = jnp.concatenate([before, x, after], axis=dim)
    return x


def layer_norm(values, gain):
    values = values.astype(jnp.float32)
    centre_mean = jnp.mean(values, axis=-1, keepdims=True)
    centred = values - centre_mean
    variance = jnp.mean(centred * centred, axis=-1, keepdims=True)
    return centred * lax.rsqrt(variance + EPSILON) * gain


def utterance_ids(lengths, first_frame, frame_count, frame_total):
    utter_ends = jnp.cumsum(lengths)
    positions = first_frame + jnp.arange(frame_count, dtype=jnp.int32)
    found = jnp.sum((positions[:, None] >= utter_ends[None, :]).astype(jnp.int32), axis=1)
    outside = jnp.where(positions < 0, -1, -2).astype(jnp.int32)
    inside = (positions >= 0) & (positions < frame_total)
    return jnp.where(inside, found, outside)


def attend_rows(query_rows, key_rows, value_rows, query_ids, key_ids):
    query_heads = query_rows.reshape(query_rows.shape[0], -1, HEAD)
    key_heads = key_rows.reshape(key_rows.shape[0], -1, HEAD)
    value_heads = value_rows.reshape(value_rows.shape[0], -1, HEAD)
    scores = jnp.einsum(
        "qhd,khd->hqk", query_heads, key_heads, preferred_element_type=jnp.float32
    ) * HEAD ** (-0.5)
    same_utter = (query_ids[:, None] == key_ids[None, :])[None]
    weights = jnp.where(same_utter, jnp.exp(scores), 0.0)
    probs = (weights / jnp.sum(weights, axis=-1, keepdims=True)).astype(jnp.bfloat16)
    mixed_rows = jnp.einsum("hqk,khd->qhd", probs, value_heads, preferred_element_type=jnp.float32)
    return mixed_rows.reshape(query_rows.shape[0], -1).astype(jnp.bfloat16)


def depthwise(window, conv_ids, conv_taps, frame_rows, margin):
    window = window.astype(jnp.float32)
    centre_ids = conv_ids[margin : margin + frame_rows]
    running = jnp.zeros((frame_rows, window.shape[1]), jnp.float32)
    for tap_index in range(conv_taps.shape[0]):
        keep_mask = (conv_ids[tap_index : tap_index + frame_rows] == centre_ids)[:, None]
        running = running + jnp.where(
            keep_mask, window[tap_index : tap_index + frame_rows] * conv_taps[tap_index], 0.0
        )
    return (running * jax.nn.sigmoid(running)).astype(jnp.bfloat16)


def body(
    frames,
    lengths,
    norm_gain,
    qkv_weight,
    out_weight,
    conv_gain,
    glu_weight,
    conv_taps,
    point_weight,
):
    frame_rows = frames.shape[0]
    model_width = frames.shape[1]
    group_cols = qkv_weight.shape[2]
    chan_cols = glu_weight.shape[2]
    out_cols = model_width // lax.axis_size("tp")
    col_start = lax.axis_index("tp") * out_cols
    frame_total = frame_rows * lax.axis_size(("seq", "dp"))
    first_frame = lax.axis_index(("seq", "dp")) * frame_rows
    normed = layer_norm(frames, norm_gain).astype(jnp.bfloat16)
    packed = jnp.dot(
        normed, qkv_weight.reshape(model_width, 3 * group_cols), preferred_element_type=jnp.float32
    ).astype(jnp.bfloat16)
    window_ids = utterance_ids(lengths, first_frame - frame_rows, 3 * frame_rows, frame_total)
    own_ids = window_ids[frame_rows : 2 * frame_rows]
    nearby = padded_2(packed[:, group_cols:], ((("seq", "dp"), 0),), frame_rows)
    mixed_rows = attend_rows(
        packed[:, :group_cols], nearby[:, :group_cols], nearby[:, group_cols:], own_ids, window_ids
    )
    partial_value = jnp.dot(mixed_rows, out_weight, preferred_element_type=jnp.float32)
    residual = frames.astype(jnp.float32) + lax.psum(
        partial_value.astype(jnp.bfloat16), "tp"
    ).astype(jnp.float32)
    normed_conv = layer_norm(residual, conv_gain).astype(jnp.bfloat16)
    own_cols = lax.dynamic_slice_in_dim(residual, col_start, out_cols, 1)
    glu_out = jnp.dot(
        normed_conv,
        glu_weight.reshape(model_width, 2 * chan_cols),
        preferred_element_type=jnp.float32,
    )
    gated_in = (glu_out[:, :chan_cols] * jax.nn.sigmoid(glu_out[:, chan_cols:])).astype(
        jnp.bfloat16
    )
    margin = KERNEL // 2
    padded = padded_2(gated_in, ((("seq", "dp"), 0),), margin)
    conv_ids = window_ids[frame_rows - margin : 2 * frame_rows + margin]
    activated = depthwise(padded, conv_ids, conv_taps, frame_rows, margin)
    conv_terms = jnp.dot(activated, point_weight, preferred_element_type=jnp.float32)
    summed = lax.psum_scatter(
        conv_terms.astype(jnp.bfloat16), "tp", scatter_dimension=1, tiled=True
    ).astype(jnp.float32)
    return (own_cols + summed).astype(jnp.bfloat16)


def solution(mesh):
    return jax.shard_map(
        body,
        mesh=mesh,
        in_specs=(
            P(("seq", "dp"), None),
            P(),
            P(),
            P(None, None, "tp"),
            P("tp", None),
            P(),
            P(None, None, "tp"),
            P(None, "tp"),
            P("tp", None),
        ),
        out_specs=P(("seq", "dp"), "tp"),
        check_vma=False,
    )
```

profile of v0, /device:TPU:6, one launch (start us, length us, event | category | flops | bytes accessed | tf_op | source)
XLA Modules:
  0.0 195.9 jit_solution(11726583221650917168)
XLA Ops:
  6.5 0.0 copy-start
  6.5 0.0 all-reduce.2.cloned.1.call-start
  6.5 1.4 convert_reduce_fusion
  8.0 1.5 fusion.3
  9.5 0.0 copy-start.1
  9.5 0.0 copy-start.45
  9.5 6.1 %copy.21 = bf16[1536,3,384]{0,2,1:T(8,128)(2,1)} copy(bf16[1536,3,384]{2,0,1:T(8,128)(2,1)} %param.12) | data formatting | bytes 7077888 | tf_op args[3]
  15.6 0.0 copy-done.1
  15.6 0.0 copy-done.45
  15.6 3.3 %convolution_convert_fusion = bf16[256,1152]{1,0:T(8,128)(2,1)S(1)} fusion(bf16[1536,1152]{0,1:T(8,128)(2,1)} %bitcast.21, bf16[256,1536]{1,0:T(8,128)(2,1)S(1)} %copy-done.1, f32[1536]{0:T(1024)S(1)} %copy-done.45, f32[256]{0:T(256)S(1)} %add_rsqrt_fusion.1, f32[256]{0:T(256)S(1)} %broadcast_multiply_fusion.1), kind=kOutput, calls=%fused_computation.2 | convolution fusion | flops 908230656 | bytes 4923392 | tf_op jit(solution)/shard_map/dot_general | solution.py:89
  18.9 1.9 collective-permute-start
  20.9 18.4 %collective-permute-start.1 = (bf16[256,768]{1,0:T(8,128)(2,1)S(1)}, bf16[256,768]{1,0:T(8,128)(2,1)}, u32[]{:S(2)}, u32[]{:S(2)}) collective-permute-start(bf16[256,768]{1,0:T(8,128)(2,1)S(1)} %slice.438), channel_id=1, source_target_pairs={{1,0},{8,1},{9,8},{16,9},{17,16},{24,17},{25,24},{32,25},{33,32},{... | collective-permute-start | bytes 1179656 | tf_op jit(solution)/shard_map/ppermute | solution.py:21
  39.3 0.0 copy-done.47
  39.3 0.2 reduce-window.8
  39.5 0.1 convert_reduce_fusion.1
  39.6 0.1 copy.23
  39.8 3.5 %copy.27 = bf16[192,8,2,384]{3,1,2,0:T(8,128)(2,1)} copy(bf16[192,8,2,384]{3,2,1,0:T(2,128)(2,1)} %bitcast.23) | data formatting | bytes 4718592
  43.3 0.6 slice_compare_fusion.26
  43.9 0.9 broadcast_compare_fusion
  44.8 0.0 collective-permute-done
  44.8 0.0 collective-permute-done.1
  44.8 1.2 pad_maximum_fusion
  46.0 0.1 fusion.90
  46.1 1.1 copy.24
  47.2 0.3 copy.22
  47.5 0.0 copy-start.4
  47.5 2.2 %fusion = (f32[4,256]{1,0:T(4,128)S(1)}, f32[4,256,768]{2,1,0:T(8,128)S(1)}) fusion(pred[256,768]{1,0:T(8,128)(4,1)} %broadcast_compare_fusion, bf16[256,4,96]{0,2,1:T(8,128)(2,1)S(1)} %bitcast.28, bf16[768,4,96]{0,2,1:T(8,128)(2,1)} %bitcast.26), kind=kOutput, calls=%fused_computation.5 | convolution fusion | flops 153353216 | bytes 4132864 | tf_op jit(solution)/shard_map/qhd,khd->hqk/dot_general | solution.py:47
  49.7 0.0 copy-done.4
  49.7 1.0 fusion.7
  50.7 0.0 copy-start.5
  50.7 0.0 copy-done
  50.7 1.5 convolution_convert_fusion.2
  52.2 0.0 all-reduce.2.cloned.1.call-update
  52.2 0.0 reduce-scatter.4.cloned.1.call-start
  52.3 0.0 copy-done.5
  52.3 0.7 slice_reduce_fusion.30
  53.0 0.7 slice_compare_fusion.29
  53.7 0.7 slice_compare_fusion.28
  54.3 0.7 slice_compare_fusion.27
  55.0 71.9 %all-reduce.2.cloned.1.call-done = bf16[256,1536]{1,0:T(8,128)(2,1)} async-done(((bf16[256,1536]{1,0:T(8,128)(2,1)}), bf16[256,1536]{1,0:T(8,128)(2,1)}) %all-reduce.2.cloned.1.call-update) | async-done | bytes 786448 | tf_op jit(solution)/shard_map/psum | solution.py:99
  127.0 1.6 convert_add_fusion
  128.6 0.0 copy-done.2
  128.6 0.4 multiply_reduce_fusion
  129.0 0.1 copy-done.3
  129.1 0.3 copy-done.46
  129.4 0.9 fusion.8
  130.3 0.0 copy-start.6
  130.4 0.0 copy-start.7
  130.4 0.0 copy-start.8
  130.4 0.0 copy-start.9
  130.4 0.0 copy-start.10
  130.4 0.0 copy-start.11
  130.7 0.1 fusion.80
  130.9 1.9 collective-permute-start.2
  132.8 5.8 %collective-permute-start.3 = (bf16[15,384]{1,0:T(8,128)(2,1)S(1)}, bf16[15,384]{1,0:T(8,128)(2,1)S(1)}, u32[]{:S(2)}, u32[]{:S(2)}) collective-permute-start(bf16[15,384]{1,0:T(8,128)(2,1)S(1)} %get-tuple-element.41), channel_id=1, source_target_pairs={{1,0},{8,1},{9,8},{16,9},{17,16},{24,17},{25,24},{32,25},{33,32},{... | collective-permute-start | bytes 34568 | tf_op jit(solution)/shard_map/ppermute | solution.py:21
  138.6 1.0 slice_reduce_fusion.29
  139.6 0.0 collective-permute-done.2
  139.6 0.3 collective-permute-done.3
  140.4 4.8 %convolution_convert_fusion.1 = bf16[256,1536]{1,0:T(8,128)(2,1)S(1)} fusion(bf16[384,1536]{1,0:T(8,128)(2,1)} %param.17, f32[286,384]{1,0:T(8,128)S(1)} %maximum_convert_fusion, f32[384]{0:T(512)S(1)} %get-tuple-element.34, f32[384]{0:T(512)S(1)} %get-tuple-element.35, f32[384]{0:T(512)S(1)} %get-tuple-element.6, f32[384]{0:T(512)S(1)} %get-tuple-element.7, ...), kind=kOutput, calls=%fused_computation.3 | convolution fusion | flops 311820288 | bytes 14233088 | tf_op jit(solution)/shard_map/dot_general | solution.py:116
  145.2 1.2 copy.25
  146.3 0.0 reduce-scatter.4.cloned.1.call-update
  146.3 40.9 %reduce-scatter.4.cloned.1.call-done = bf16[384,256]{1,0:T(8,128)(2,1)} async-done(((bf16[1536,256]{1,0:T(8,128)(2,1)}), bf16[384,256]{1,0:T(8,128)(2,1)}) %reduce-scatter.4.cloned.1.call-update) | async-done | bytes 196624
  187.2 1.1 copy.26
  188.3 0.7 add_convert_fusion
  (87 shorter events, 0.3 us)
Async XLA Ops:
  6.5 44.2 %copy-start = (bf16[384,1536]{1,0:T(8,128)(2,1)S(1)}, bf16[384,1536]{1,0:T(8,128)(2,1)}, u32[]{:S(2)}) copy-start(bf16[384,1536]{1,0:T(8,128)(2,1)} %param.13) | copy-start | bytes 3538948
  6.5 120.4 %all-reduce.2.cloned.1.call-start = ((), (), s32[]{:S(2)}) async-start(), calls=%async_computation.1 | async-start | bytes 1572864 | tf_op jit(solution)/shard_map/psum | solution.py:99
  9.5 6.2 %copy-start.1 = (bf16[256,1536]{1,0:T(8,128)(2,1)S(1)}, bf16[256,1536]{1,0:T(8,128)(2,1)}, u32[]{:S(2)}) copy-start(bf16[256,1536]{1,0:T(8,128)(2,1)} %param.9) | copy-start | bytes 2359300
  9.5 6.2 %copy-start.45 = (f32[1536]{0:T(1024)S(1)}, f32[1536]{0:T(1024)}, u32[]{:S(2)}) copy-start(f32[1536]{0:T(1024)} %param.11) | copy-start | bytes 18436
  15.6 23.7 %copy-start.47 = (s32[4]{0:T(128)S(1)}, s32[4]{0:T(128)}, u32[]{:S(2)}) copy-start(s32[4]{0:T(128)} %param.10) | copy-start | bytes 52
  18.9 25.9 %collective-permute-start = (bf16[256,768]{1,0:T(8,128)(2,1)S(1)}, bf16[256,768]{1,0:T(8,128)(2,1)}, u32[]{:S(2)}, u32[]{:S(2)}) collective-permute-start(bf16[256,768]{1,0:T(8,128)(2,1)S(1)} %slice.438), channel_id=1, source_target_pairs={{0,1},{1,8},{8,9},{9,16},{16,17},{17,24},{24,25},{25,32},{32,33},{... | collective-permute-start | bytes 1179656 | tf_op jit(solution)/shard_map/ppermute | solution.py:20
  20.9 23.9 %collective-permute-start.1 = (bf16[256,768]{1,0:T(8,128)(2,1)S(1)}, bf16[256,768]{1,0:T(8,128)(2,1)}, u32[]{:S(2)}, u32[]{:S(2)}) collective-permute-start(bf16[256,768]{1,0:T(8,128)(2,1)S(1)} %slice.438), channel_id=1, source_target_pairs={{1,0},{8,1},{9,8},{16,9},{17,16},{24,17},{25,24},{32,25},{33,32},{... | collective-permute-start | bytes 1179656 | tf_op jit(solution)/shard_map/ppermute | solution.py:21
  47.5 2.2 %copy-start.4 = (pred[256,768]{1,0:T(8,128)(4,1)S(1)}, pred[256,768]{1,0:T(8,128)(4,1)}, u32[]{:S(2)}) copy-start(pred[256,768]{1,0:T(8,128)(4,1)} %broadcast_compare_fusion) | copy-start | bytes 589828
  50.7 1.6 copy-start.5
  52.2 135.0 %reduce-scatter.4.cloned.1.call-start = ((), (), s32[]{:S(2)}) async-start(), calls=%async_computation.2 | async-start | bytes 983040
  127.0 1.6 copy-start.2
  127.0 2.2 %copy-start.3 = (bf16[192,8,2,384]{3,1,2,0:T(8,128)(2,1)S(1)}, bf16[192,8,2,384]{3,1,2,0:T(8,128)(2,1)}, u32[]{:S(2)}) copy-start(bf16[192,8,2,384]{3,1,2,0:T(8,128)(2,1)} %copy.27) | copy-start | bytes 7077892
  128.6 0.8 copy-start.46
  130.3 9.7 %copy-start.6 = (f32[384]{0:T(512)S(1)}, f32[384]{0:T(512)}, u32[]{:S(2)}) copy-start(f32[384]{0:T(512)} %get-tuple-element.9) | copy-start | bytes 4612
  130.4 9.7 %copy-start.7 = (f32[384]{0:T(512)S(1)}, f32[384]{0:T(512)}, u32[]{:S(2)}) copy-start(f32[384]{0:T(512)} %get-tuple-element.10) | copy-start | bytes 4612
  130.4 9.7 %copy-start.8 = (f32[384]{0:T(512)S(1)}, f32[384]{0:T(512)}, u32[]{:S(2)}) copy-start(f32[384]{0:T(512)} %get-tuple-element.11) | copy-start | bytes 4612
  130.4 9.7 %copy-start.9 = (f32[384]{0:T(512)S(1)}, f32[384]{0:T(512)}, u32[]{:S(2)}) copy-start(f32[384]{0:T(512)} %get-tuple-element.12) | copy-start | bytes 4612
  130.4 9.7 %copy-start.10 = (f32[384]{0:T(512)S(1)}, f32[384]{0:T(512)}, u32[]{:S(2)}) copy-start(f32[384]{0:T(512)} %get-tuple-element.13) | copy-start | bytes 4612
  130.4 9.7 %copy-start.11 = (f32[384]{0:T(512)S(1)}, f32[384]{0:T(512)}, u32[]{:S(2)}) copy-start(f32[384]{0:T(512)} %get-tuple-element.14) | copy-start | bytes 4612
  130.4 9.7 %copy-start.12 = (f32[384]{0:T(512)S(1)}, f32[384]{0:T(512)}, u32[]{:S(2)}) copy-start(f32[384]{0:T(512)} %get-tuple-element.15) | copy-start | bytes 4612
  130.4 9.7 %copy-start.13 = (f32[384]{0:T(512)S(1)}, f32[384]{0:T(512)}, u32[]{:S(2)}) copy-start(f32[384]{0:T(512)} %get-tuple-element.16) | copy-start | bytes 4612
  130.4 9.7 %copy-start.14 = (f32[384]{0:T(512)S(1)}, f32[384]{0:T(512)}, u32[]{:S(2)}) copy-start(f32[384]{0:T(512)} %get-tuple-element.17) | copy-start | bytes 4612
  130.4 9.7 %copy-start.15 = (f32[384]{0:T(512)S(1)}, f32[384]{0:T(512)}, u32[]{:S(2)}) copy-start(f32[384]{0:T(512)} %get-tuple-element.18) | copy-start | bytes 4612
  130.4 9.7 %copy-start.16 = (f32[384]{0:T(512)S(1)}, f32[384]{0:T(512)}, u32[]{:S(2)}) copy-start(f32[384]{0:T(512)} %get-tuple-element.19) | copy-start | bytes 4612
  130.5 9.7 %copy-start.17 = (f32[384]{0:T(512)S(1)}, f32[384]{0:T(512)}, u32[]{:S(2)}) copy-start(f32[384]{0:T(512)} %get-tuple-element.20) | copy-start | bytes 4612
  130.5 9.7 %copy-start.18 = (f32[384]{0:T(512)S(1)}, f32[384]{0:T(512)}, u32[]{:S(2)}) copy-start(f32[384]{0:T(512)} %get-tuple-element.21) | copy-start | bytes 4612
  130.5 9.7 %copy-start.19 = (f32[384]{0:T(512)S(1)}, f32[384]{0:T(512)}, u32[]{:S(2)}) copy-start(f32[384]{0:T(512)} %get-tuple-element.22) | copy-start | bytes 4612
  130.5 9.7 %copy-start.20 = (f32[384]{0:T(512)S(1)}, f32[384]{0:T(512)}, u32[]{:S(2)}) copy-start(f32[384]{0:T(512)} %get-tuple-element.23) | copy-start | bytes 4612
  130.5 9.7 %copy-start.21 = (pred[256]{0:T(512)(128)(4,1)S(1)}, pred[256]{0:T(512)(128)(4,1)}, u32[]{:S(2)}) copy-start(pred[256]{0:T(512)(128)(4,1)} %get-tuple-element.69) | copy-start | bytes 772
  130.5 9.7 %copy-start.22 = (pred[256]{0:T(512)(128)(4,1)S(1)}, pred[256]{0:T(512)(128)(4,1)}, u32[]{:S(2)}) copy-start(pred[256]{0:T(512)(128)(4,1)} %get-tuple-element.70) | copy-start | bytes 772
  130.5 9.7 %copy-start.23 = (pred[256]{0:T(512)(128)(4,1)S(1)}, pred[256]{0:T(512)(128)(4,1)}, u32[]{:S(2)}) copy-start(pred[256]{0:T(512)(128)(4,1)} %get-tuple-element.71) | copy-start | bytes 772
  130.5 9.7 %copy-start.24 = (pred[256]{0:T(512)(128)(4,1)S(1)}, pred[256]{0:T(512)(128)(4,1)}, u32[]{:S(2)}) copy-start(pred[256]{0:T(512)(128)(4,1)} %get-tuple-element.42) | copy-start | bytes 772
  130.5 9.7 %copy-start.25 = (pred[256]{0:T(512)(128)(4,1)S(1)}, pred[256]{0:T(512)(128)(4,1)}, u32[]{:S(2)}) copy-start(pred[256]{0:T(512)(128)(4,1)} %get-tuple-element.43) | copy-start | bytes 772
  130.5 9.7 %copy-start.26 = (pred[256]{0:T(512)(128)(4,1)S(1)}, pred[256]{0:T(512)(128)(4,1)}, u32[]{:S(2)}) copy-start(pred[256]{0:T(512)(128)(4,1)} %get-tuple-element.44) | copy-start | bytes 772
  130.6 9.7 %copy-start.27 = (pred[256]{0:T(512)(128)(4,1)S(1)}, pred[256]{0:T(512)(128)(4,1)}, u32[]{:S(2)}) copy-start(pred[256]{0:T(512)(128)(4,1)} %get-tuple-element.45) | copy-start | bytes 772
  130.6 9.7 %copy-start.28 = (pred[256]{0:T(512)(128)(4,1)S(1)}, pred[256]{0:T(512)(128)(4,1)}, u32[]{:S(2)}) copy-start(pred[256]{0:T(512)(128)(4,1)} %get-tuple-element.46) | copy-start | bytes 772
  130.6 9.7 %copy-start.29 = (pred[256]{0:T(512)(128)(4,1)S(1)}, pred[256]{0:T(512)(128)(4,1)}, u32[]{:S(2)}) copy-start(pred[256]{0:T(512)(128)(4,1)} %get-tuple-element.47) | copy-start | bytes 772
  130.6 9.7 %copy-start.30 = (pred[256]{0:T(512)(128)(4,1)S(1)}, pred[256]{0:T(512)(128)(4,1)}, u32[]{:S(2)}) copy-start(pred[256]{0:T(512)(128)(4,1)} %get-tuple-element.48) | copy-start | bytes 772
  130.6 9.7 %copy-start.31 = (pred[256]{0:T(512)(128)(4,1)S(1)}, pred[256]{0:T(512)(128)(4,1)}, u32[]{:S(2)}) copy-start(pred[256]{0:T(512)(128)(4,1)} %get-tuple-element.49) | copy-start | bytes 772
  130.6 9.7 %copy-start.32 = (pred[256]{0:T(512)(128)(4,1)S(1)}, pred[256]{0:T(512)(128)(4,1)}, u32[]{:S(2)}) copy-start(pred[256]{0:T(512)(128)(4,1)} %get-tuple-element.50) | copy-start | bytes 772
  130.6 9.7 %copy-start.33 = (pred[256]{0:T(512)(128)(4,1)S(1)}, pred[256]{0:T(512)(128)(4,1)}, u32[]{:S(2)}) copy-start(pred[256]{0:T(512)(128)(4,1)} %get-tuple-element.51) | copy-start | bytes 772
  130.6 9.7 %copy-start.34 = (pred[256]{0:T(512)(128)(4,1)S(1)}, pred[256]{0:T(512)(128)(4,1)}, u32[]{:S(2)}) copy-start(pred[256]{0:T(512)(128)(4,1)} %get-tuple-element.52) | copy-start | bytes 772
  130.6 9.7 %copy-start.35 = (pred[256]{0:T(512)(128)(4,1)S(1)}, pred[256]{0:T(512)(128)(4,1)}, u32[]{:S(2)}) copy-start(pred[256]{0:T(512)(128)(4,1)} %get-tuple-element.53) | copy-start | bytes 772
  130.6 9.7 %copy-start.36 = (pred[256]{0:T(512)(128)(4,1)S(1)}, pred[256]{0:T(512)(128)(4,1)}, u32[]{:S(2)}) copy-start(pred[256]{0:T(512)(128)(4,1)} %get-tuple-element.54) | copy-start | bytes 772
  130.7 9.7 %copy-start.37 = (pred[256]{0:T(512)(128)(4,1)S(1)}, pred[256]{0:T(512)(128)(4,1)}, u32[]{:S(2)}) copy-start(pred[256]{0:T(512)(128)(4,1)} %get-tuple-element.55) | copy-start | bytes 772
  130.7 9.7 %copy-start.38 = (pred[256]{0:T(512)(128)(4,1)S(1)}, pred[256]{0:T(512)(128)(4,1)}, u32[]{:S(2)}) copy-start(pred[256]{0:T(512)(128)(4,1)} %get-tuple-element.56) | copy-start | bytes 772
  130.7 9.7 %copy-start.39 = (pred[256]{0:T(512)(128)(4,1)S(1)}, pred[256]{0:T(512)(128)(4,1)}, u32[]{:S(2)}) copy-start(pred[256]{0:T(512)(128)(4,1)} %get-tuple-element.57) | copy-start | bytes 772
  130.7 9.7 %copy-start.40 = (pred[256]{0:T(512)(128)(4,1)S(1)}, pred[256]{0:T(512)(128)(4,1)}, u32[]{:S(2)}) copy-start(pred[256]{0:T(512)(128)(4,1)} %get-tuple-element.58) | copy-start | bytes 772
  130.7 9.7 %copy-start.41 = (pred[256]{0:T(512)(128)(4,1)S(1)}, pred[256]{0:T(512)(128)(4,1)}, u32[]{:S(2)}) copy-start(pred[256]{0:T(512)(128)(4,1)} %get-tuple-element.59) | copy-start | bytes 772
  130.7 9.7 %copy-start.42 = (pred[256]{0:T(512)(128)(4,1)S(1)}, pred[256]{0:T(512)(128)(4,1)}, u32[]{:S(2)}) copy-start(pred[256]{0:T(512)(128)(4,1)} %get-tuple-element.60) | copy-start | bytes 772
  130.7 9.7 %copy-start.43 = (pred[256]{0:T(512)(128)(4,1)S(1)}, pred[256]{0:T(512)(128)(4,1)}, u32[]{:S(2)}) copy-start(pred[256]{0:T(512)(128)(4,1)} %get-tuple-element.61) | copy-start | bytes 772
  130.7 9.7 %copy-start.44 = (pred[256]{0:T(512)(128)(4,1)S(1)}, pred[256]{0:T(512)(128)(4,1)}, u32[]{:S(2)}) copy-start(pred[256]{0:T(512)(128)(4,1)} %get-tuple-element.62) | copy-start | bytes 772
  130.9 8.7 %collective-permute-start.2 = (bf16[15,384]{1,0:T(8,128)(2,1)S(1)}, bf16[15,384]{1,0:T(8,128)(2,1)S(1)}, u32[]{:S(2)}, u32[]{:S(2)}) collective-permute-start(bf16[15,384]{1,0:T(8,128)(2,1)S(1)} %get-tuple-element.40), channel_id=1, source_target_pairs={{0,1},{1,8},{8,9},{9,16},{16,17},{17,24},{24,25},{25,32},{32,33},{... | collective-permute-start | bytes 34568 | tf_op jit(solution)/shard_map/ppermute | solution.py:20
  132.8 7.1 %collective-permute-start.3 = (bf16[15,384]{1,0:T(8,128)(2,1)S(1)}, bf16[15,384]{1,0:T(8,128)(2,1)S(1)}, u32[]{:S(2)}, u32[]{:S(2)}) collective-permute-start(bf16[15,384]{1,0:T(8,128)(2,1)S(1)} %get-tuple-element.41), channel_id=1, source_target_pairs={{1,0},{8,1},{9,8},{16,9},{17,16},{24,17},{25,24},{32,25},{33,32},{... | collective-permute-start | bytes 34568 | tf_op jit(solution)/shard_map/ppermute | solution.py:21
Sparse Core Ops, SparseCore 0:
  52.3 74.5 all-reduce.1
  146.4 40.7 reduce-scatter.3
where the time goes:
time: 197 us; the launch traced here: 196 us
  waiting for transfers between devices  113 us (57%)
  starting transfers between devices  28 us (14%)
  local copies, waits for them, and re-layouts  16 us (8%)
  between operations  14.3 us (7%)
  matrix products  13.6 us (7%)
  other arithmetic  10.8 us (5%)
    psum x1, waiting for transfers between devices, body(): lax.psum(partial_value.astype(jnp.bfloat16), 'tp').astype(jnp.float32)  71.9 us
    unnamed x3, waiting for transfers between devices  40.9 us
    ppermute x2, starting transfers between devices, padded_2(): after = lax.ppermute(initial, axis, down)  24.1 us
    unnamed x100, local copies, waits for them, and re-layouts  12.5 us
    dot_general x1, matrix products, body(): jnp.dot(activated, point_weight, preferred_element_type=jnp.float32)  4.76 us
  transfers between devices with their start and end apart: 6, of which 3 were waited for; matrix products, arithmetic and copies ran while one was open for 5% of the time, Pallas kernels for 0%

commit v1 on v0

v1 whole, which is shorter than its diff:
```python
import jax
import jax.numpy as jnp
from jax import lax
from jax.experimental import pallas as pl
from jax.experimental.pallas import tpu as pltpu
from jax.sharding import PartitionSpec as P

HEAD = 96
KERNEL = 31
MARGIN = KERNEL // 2
HALO = 16
LANES = 128
EPSILON = 1e-05
LOG2E = 1.4426950408889634

VMEM = pl.BlockSpec(memory_space=pltpu.VMEM)
SMEM = pl.BlockSpec(memory_space=pltpu.SMEM)


def params():
    return pltpu.CompilerParams(vmem_limit_bytes=48 * 1024 * 1024)


def cost(flops, size, transcendentals=0):
    return pl.CostEstimate(flops=flops, bytes_accessed=size, transcendentals=transcendentals)


def along_stream(x, step):
    axes = ("seq", "dp")
    devices = lax.axis_size(axes)
    pairs = [(i, i + step) for i in range(devices) if 0 <= i + step < devices]
    return lax.ppermute(x, axes, pairs)


def matmul(left, right):
    return jnp.dot(left, right, preferred_element_type=jnp.float32)


def first_row(rows):
    return (lax.axis_index("seq") * lax.axis_size("dp") + lax.axis_index("dp")) * rows


def ends_of(lengths_ref):
    ends, total = [], jnp.int32(0)
    for i in range(lengths_ref.shape[0]):
        total = total + lengths_ref[i]
        ends.append(total)
    return ends


def ids_of(positions, ends):
    found = jnp.zeros_like(positions)
    for end in ends:
        found = found + (positions >= end).astype(jnp.int32)
    return jnp.where(positions < 0, -1, found)


def project_kernel(frames_ref, gain_ref, weight_ref, normed_ref, out_ref):
    @pl.when(pl.program_id(0) == 0)
    def _():
        values = frames_ref[...].astype(jnp.float32)
        centred = values - jnp.mean(values, axis=-1, keepdims=True)
        variance = jnp.mean(centred * centred, axis=-1, keepdims=True)
        normed_ref[...] = (centred * lax.rsqrt(variance + EPSILON) * gain_ref[...]).astype(jnp.bfloat16)

    out_ref[...] = matmul(normed_ref[...], weight_ref[0]).astype(jnp.bfloat16)


def query_kernel(normed_ref, weight_ref, out_ref):
    out_ref[...] = matmul(normed_ref[...], weight_ref[0]).astype(jnp.bfloat16)


def attend_kernel(lengths_ref, query_ref, before_ref, own_ref, after_ref, weight_ref, out_ref):
    rows, cols = query_ref.shape
    heads = cols // HEAD
    start = first_row(rows)
    ends = ends_of(lengths_ref)
    query_ids = ids_of(start + lax.broadcasted_iota(jnp.int32, (rows, 1), 0), ends)
    sides = (before_ref, own_ref, after_ref)
    same = []
    for side in range(3):
        at = start + (side - 1) * rows
        same.append(query_ids == ids_of(at + lax.broadcasted_iota(jnp.int32, (1, rows), 1), ends))
    scale = HEAD ** (-0.5) * LOG2E
    lane_groups = [None] * (cols // LANES)
    for head in range(heads):
        low, high = head * HEAD, (head + 1) * HEAD
        left, right = low // LANES * LANES, -(-high // LANES) * LANES
        lane = left + lax.broadcasted_iota(jnp.int32, (1, right - left), 1)
        mine = (lane >= low) & (lane < high)
        query = jnp.where(mine, query_ref[:, left:right], jnp.zeros((), jnp.bfloat16))
        weights, total = [], None
        for side in range(3):
            scores = lax.dot_general(
                query,
                sides[side][:, left:right],
                (((1,), (1,)), ((), ())),
                preferred_element_type=jnp.float32,
            )
            piece = jnp.where(same[side], jnp.exp2(scores * scale), 0.0)
            weights.append(piece)
            part = jnp.sum(piece, axis=-1, keepdims=True)
            total = part if total is None else total + part
        shift = jnp.where(total > 1.0, 2.0**-20, 2.0**20)
        inverse = 1.0 / (total * shift)
        mixed = None
        for side in range(3):
            probs = (weights[side] * inverse * shift).astype(jnp.bfloat16)
            term = matmul(probs, sides[side][:, cols + left : cols + right])
            mixed = term if mixed is None else mixed + term
        for group in range(left // LANES, right // LANES):
            lanes = slice(group * LANES - left, (group + 1) * LANES - left)
            old, new = lane_groups[group], mixed[:, lanes]
            lane_groups[group] = new if old is None else jnp.where(mine[:, lanes], new, old)
    mixed_rows = jnp.concatenate([x.astype(jnp.bfloat16) for x in lane_groups], axis=1)
    chunks, _, width = out_ref.shape
    for chunk in range(chunks):
        part = matmul(mixed_rows, weight_ref[:, chunk * width : (chunk + 1) * width])
        out_ref[chunk] = part.astype(jnp.bfloat16)


def glu_kernel(residual_ref, gain_ref, weight_ref, out_ref):
    chunks, _, width = residual_ref.shape
    model_width = chunks * width
    parts = [residual_ref[i].astype(jnp.float32) for i in range(chunks)]
    mean = sum(jnp.sum(x, axis=-1, keepdims=True) for x in parts) / model_width
    parts = [x - mean for x in parts]
    variance = sum(jnp.sum(x * x, axis=-1, keepdims=True) for x in parts) / model_width
    inverse = lax.rsqrt(variance + EPSILON)
    value = gate = None
    for i in range(chunks):
        span = slice(i * width, (i + 1) * width)
        normed = (parts[i] * inverse * gain_ref[:, span]).astype(jnp.bfloat16)
        value_term = matmul(normed, weight_ref[0, span])
        gate_term = matmul(normed, weight_ref[1, span])
        value = value_term if value is None else value + value_term
        gate = gate_term if gate is None else gate + gate_term
    out_ref[...] = (value * jax.nn.sigmoid(gate)).astype(jnp.bfloat16)


def conv_kernel(lengths_ref, before_ref, own_ref, after_ref, taps_ref, weight_ref, out_ref, window_ref):
    rows, cols = own_ref.shape
    start = first_row(rows)
    ends = ends_of(lengths_ref)
    positions = start + lax.broadcasted_iota(jnp.int32, (rows, LANES), 0)
    first = jnp.zeros_like(positions)
    last = jnp.zeros_like(positions)
    begin = jnp.int32(0)
    for end in ends:
        inside = (positions >= begin) & (positions < end)
        first = jnp.where(inside, begin - positions, first)
        last = jnp.where(inside, end - 1 - positions, last)
        begin = end
    window_ref[:HALO] = before_ref[...].astype(jnp.float32)
    window_ref[HALO : HALO + rows] = own_ref[...].astype(jnp.float32)
    window_ref[HALO + rows :] = after_ref[...].astype(jnp.float32)
    step = 64
    activated = []
    for row in range(0, rows, step):
        groups = []
        low, high = first[row : row + step], last[row : row + step]
        for lane in range(0, cols, LANES):
            running = jnp.zeros((step, LANES), jnp.float32)
            for tap in range(KERNEL):
                offset = tap - MARGIN
                at = HALO + offset + row
                term = window_ref[at : at + step, lane : lane + LANES] * taps_ref[tap : tap + 1, lane : lane + LANES]
                if offset:
                    keep = (low <= offset) if offset < 0 else (high >= offset)
                    term = jnp.where(keep, term, 0.0)
                running = running + term
            groups.append((running * jax.nn.sigmoid(running)).astype(jnp.bfloat16))
        activated.append(jnp.concatenate(groups, axis=1))
    activated = jnp.concatenate(activated, axis=0)
    chunks, _, width = out_ref.shape
    for chunk in range(chunks):
        part = matmul(activated, weight_ref[:, chunk * width : (chunk + 1) * width])
        out_ref[chunk] = part.astype(jnp.bfloat16)


def body(
    frames,
    lengths,
    norm_gain,
    qkv_weight,
    out_weight,
    conv_gain,
    glu_weight,
    conv_taps,
    point_weight,
):
    rows, model_width = frames.shape
    group_cols = qkv_weight.shape[2]
    chan_cols = glu_weight.shape[2]
    parts = lax.axis_size("tp")
    out_cols = model_width // parts
    bf16 = jnp.bfloat16
    qkv = jnp.swapaxes(qkv_weight, 0, 1)

    normed, keys_values = pl.pallas_call(
        project_kernel,
        grid=(2,),
        in_specs=[
            pl.BlockSpec((rows, model_width), lambda i: (0, 0)),
            pl.BlockSpec((1, model_width), lambda i: (0, 0)),
            pl.BlockSpec((1, model_width, group_cols), lambda i: (i + 1, 0, 0)),
        ],
        out_specs=[
            pl.BlockSpec((rows, model_width), lambda i: (0, 0)),
            pl.BlockSpec((rows, group_cols), lambda i: (0, i)),
        ],
        out_shape=[
            jax.ShapeDtypeStruct((rows, model_width), bf16),
            jax.ShapeDtypeStruct((rows, 2 * group_cols), bf16),
        ],
        compiler_params=params(),
        cost_estimate=cost(4 * rows * model_width * group_cols, 4_000_000),
        name="project",
    )(frames, norm_gain[None], qkv)
    before = along_stream(keys_values, 1)
    after = along_stream(keys_values, -1)
    query = pl.pallas_call(
        query_kernel,
        grid=(1,),
        in_specs=[
            pl.BlockSpec((rows, model_width), lambda i: (0, 0)),
            pl.BlockSpec((1, model_width, group_cols), lambda i: (0, 0, 0)),
        ],
        out_specs=pl.BlockSpec((rows, group_cols), lambda i: (0, 0)),
        out_shape=jax.ShapeDtypeStruct((rows, group_cols), bf16),
        compiler_params=params(),
        cost_estimate=cost(2 * rows * model_width * group_cols, 2_200_000),
        name="query",
    )(normed, qkv)
    attn_terms = pl.pallas_call(
        attend_kernel,
        in_specs=[SMEM] + [VMEM] * 5,
        out_specs=VMEM,
        out_shape=jax.ShapeDtypeStruct((parts, rows, out_cols), bf16),
        compiler_params=params(),
        cost_estimate=cost(10**9, 4_000_000, 4 * 3 * rows * rows),
        name="attend",
    )(lengths, query, before, keys_values, after, out_weight)
    attn_terms = lax.all_to_all(attn_terms, "tp", 0, 0, tiled=True)
    own_frames = lax.dynamic_slice_in_dim(frames, lax.axis_index("tp") * out_cols, out_cols, 1)
    residual = own_frames.astype(jnp.float32) + jnp.sum(attn_terms.astype(jnp.float32), axis=0)
    gathered = lax.all_gather(residual.astype(bf16), "tp", axis=0)
    gated = pl.pallas_call(
        glu_kernel,
        in_specs=[VMEM] * 3,
        out_specs=VMEM,
        out_shape=jax.ShapeDtypeStruct((rows, chan_cols), bf16),
        compiler_params=params(),
        cost_estimate=cost(4 * rows * model_width * chan_cols, 3_500_000),
        name="glu",
    )(gathered, conv_gain[None], jnp.swapaxes(glu_weight, 0, 1))
    conv_before = along_stream(gated[rows - HALO :], 1)
    conv_after = along_stream(gated[:HALO], -1)
    conv_terms = pl.pallas_call(
        conv_kernel,
        in_specs=[SMEM] + [VMEM] * 5,
        out_specs=VMEM,
        out_shape=jax.ShapeDtypeStruct((parts, rows, out_cols), bf16),
        scratch_shapes=[pltpu.VMEM((rows + 2 * HALO, chan_cols), jnp.float32)],
        compiler_params=params(),
        cost_estimate=cost(2 * rows * model_width * chan_cols, 2_500_000),
        name="conv",
    )(lengths, conv_before, gated, conv_after, conv_taps, point_weight)
    conv_terms = lax.all_to_all(conv_terms, "tp", 0, 0, tiled=True)
    return (residual + jnp.sum(conv_terms.astype(jnp.float32), axis=0)).astype(bf16)


def solution(mesh):
    return jax.shard_map(
        body,
        mesh=mesh,
        in_specs=(
            P(("seq", "dp"), None),
            P(),
            P(),
            P(None, None, "tp"),
            P("tp", None),
            P(),
            P(None, None, "tp"),
            P(None, "tp"),
            P("tp", None),
        ),
        out_specs=P(("seq", "dp"), "tp"),
        check_vma=False,
    )
```

time: 197 us -> 97.1 us (0.49)
  waiting for transfers between devices: 113 us -> 22.2 us
  blocking collectives: 0 us -> 25.7 us
  between operations: 14.3 us -> 0.14 us
  matrix products: 13.6 us -> 0 us
  Pallas kernels: 0 us -> 11.1 us
  local copies, waits for them, and re-layouts: 16 us -> 5.92 us
  other arithmetic: 10.8 us -> 2.19 us
    psum x1 -> x0, waiting for transfers between devices: 71.9 us -> none  [body(): lax.psum(partial_value.astype(jnp.bfloat16), 'tp').astype(jnp.float32)]
    unnamed x3 -> x0, waiting for transfers between devices: 40.9 us -> none
    dot_general x6 -> x0, matrix products: 13.6 us -> none  [the longest x1 4.76 us: body(): jnp.dot(activated, point_weight, preferred_element_type=jnp.float32)]
    all_gather x0 -> x1, blocking collectives: none -> 13.3 us  [body(): gathered = lax.all_gather(residual.astype(bf16), 'tp', axis=0)]
    ppermute x4, waiting for transfers between devices: 0.33 us -> 13.4 us  [along_stream(): return lax.ppermute(x, axes, pairs)]
    all_to_all x0 -> x1, blocking collectives: none -> 12.4 us  [body(): conv_terms = lax.all_to_all(conv_terms, 'tp', 0, 0, tiled=True)]
    pallas_call x0 -> x5, Pallas kernels: none -> 11.1 us  [the longest x1 3.93 us: body(): pl.pallas_call(conv_kernel, in_specs=[SMEM] + [VMEM] * 5, out_specs=VMEM,...]
    all_to_all x0 -> x1, waiting for transfers between devices: none -> 8.88 us  [body(): attn_terms = lax.all_to_all(attn_terms, 'tp', 0, 0, tiled=True)]
  transfers between devices with their start and end apart: 6 -> 5, of which waited for: 3 -> 4; matrix products, arithmetic and copies ran while one was open for 5% -> 2% of each run, Pallas kernels for 0% -> 1%
where the time goes in v1:
time: 97.1 us; the launch traced here: 96.6 us
  starting transfers between devices  29.2 us (30%)
  blocking collectives  25.7 us (26%)
  waiting for transfers between devices  22.2 us (23%)
  Pallas kernels  11.1 us (11%)
  local copies, waits for them, and re-layouts  5.92 us (6%)
  other arithmetic  2.19 us (2%)
    ppermute x4, starting transfers between devices, along_stream(): return lax.ppermute(x, axes, pairs)  24.6 us
    ppermute x4, waiting for transfers between devices, along_stream(): return lax.ppermute(x, axes, pairs)  13.4 us
    all_gather x1, blocking collectives, body(): gathered = lax.all_gather(residual.astype(bf16), 'tp', axis=0)  13.3 us
    all_to_all x1, blocking collectives, body(): conv_terms = lax.all_to_all(conv_terms, 'tp', 0, 0, tiled=True)  12.4 us
    all_to_all x1, waiting for transfers between devices, body(): attn_terms = lax.all_to_all(attn_terms, 'tp', 0, 0, tiled=True)  8.88 us
    unnamed x19, local copies, waits for them, and re-layouts  5.21 us
    all_to_all x1, starting transfers between devices, body(): attn_terms = lax.all_to_all(attn_terms, 'tp', 0, 0, tiled=True)  4.6 us
    pallas_call x1, Pallas kernels, body(): pl.pallas_call(conv_kernel, in_specs=[SMEM] + [VMEM] * 5, out_specs=VMEM,...  3.93 us
  transfers between devices with their start and end apart: 5, of which 4 were waited for; matrix products, arithmetic and copies ran while one was open for 2% of the time, Pallas kernels for 1%

profile of v1, /device:TPU:6, one launch (start us, length us, event | category | flops | bytes accessed | tf_op | source)
XLA Modules:
  0.0 96.6 jit_solution(7107255201263715881)
XLA Ops:
  0.0 0.7 broadcast_in_dim.6.gain_ref
  0.7 0.0 copy-start
  0.7 2.0 %copy-done = bf16[1536,3,384]{2,0,1:T(8,128)(2,1)S(1)} copy-done((bf16[1536,3,384]{2,0,1:T(8,128)(2,1)S(1)}, bf16[1536,3,384]{2,0,1:T(8,128)(2,1)}, u32[]{:S(2)}) %copy-start) | copy-done | bytes 3538968
  2.7 0.0 copy-start.2
  2.7 1.1 %copy-done.2 = bf16[256,1536]{1,0:T(8,128)(2,1)S(1)} copy-done((bf16[256,1536]{1,0:T(8,128)(2,1)S(1)}, bf16[256,1536]{1,0:T(8,128)(2,1)}, u32[]{:S(2)}) %copy-start.2) | copy-done | bytes 786456
  3.8 0.0 copy-start.1
  3.8 1.7 %project.1 = (bf16[256,1536]{1,0:T(8,128)(2,1)S(1)}, bf16[256,768]{1,0:T(8,128)(2,1)S(1)}) custom-call(bf16[256,1536]{1,0:T(8,128)(2,1)S(1)} %copy-done.2, f32[1,1536]{1,0:T(1,128)S(1)} %broadcast_in_dim.6.gain_ref, bf16[3,1536,384]{2,1,0:T(8,128)(2,1)S(1)} %bitcast.5), custom_call_target="tpu_custom_call" | custom-call | flops 603979776 | bytes 4000000 | tf_op jit(solution)/shard_map/project/pallas_call | solution.py:200
  5.5 18.4 %collective-permute-start.1 = (bf16[256,768]{1,0:T(8,128)(2,1)S(1)}, bf16[256,768]{1,0:T(8,128)(2,1)S(1)}, u32[]{:S(2)}, u32[]{:S(2)}) collective-permute-start(bf16[256,768]{1,0:T(8,128)(2,1)S(1)} %get-tuple-element.8.own_ref), channel_id=1, source_target_pairs={{1,0},{8,1},{9,8},{16,9},{17,16},{24,17},{25,24},{32,25},{33,32},{... | collective-permute-start | bytes 1179656 | tf_op jit(solution)/shard_map/ppermute | solution.py:32
  23.9 1.9 %collective-permute-start = (bf16[256,768]{1,0:T(8,128)(2,1)S(1)}, bf16[256,768]{1,0:T(8,128)(2,1)S(1)}, u32[]{:S(2)}, u32[]{:S(2)}) collective-permute-start(bf16[256,768]{1,0:T(8,128)(2,1)S(1)} %get-tuple-element.8.own_ref), channel_id=1, source_target_pairs={{0,1},{1,8},{8,9},{9,16},{16,17},{17,24},{24,25},{25,32},{32,33},{... | collective-permute-start | bytes 1179656 | tf_op jit(solution)/shard_map/ppermute | solution.py:32
  25.9 0.0 copy-done.1
  25.9 0.0 copy-start.6
  25.9 0.0 copy-start.7
  25.9 0.6 query.1.query_ref
  26.5 2.7 %collective-permute-done.1.after_ref = bf16[256,768]{1,0:T(8,128)(2,1)S(1)} collective-permute-done((bf16[256,768]{1,0:T(8,128)(2,1)S(1)}, bf16[256,768]{1,0:T(8,128)(2,1)S(1)}, u32[]{:S(2)}, u32[]{:S(2)}) %collective-permute-start.1) | collective-permute-done | bytes 393248 | tf_op jit(solution)/shard_map/ppermute | solution.py:32
  29.2 5.9 %collective-permute-done.before_ref = bf16[256,768]{1,0:T(8,128)(2,1)S(1)} collective-permute-done((bf16[256,768]{1,0:T(8,128)(2,1)S(1)}, bf16[256,768]{1,0:T(8,128)(2,1)S(1)}, u32[]{:S(2)}, u32[]{:S(2)}) %collective-permute-start) | collective-permute-done | bytes 393248 | tf_op jit(solution)/shard_map/ppermute | solution.py:32
  35.1 0.0 copy-done.6
  35.1 0.0 copy-done.7
  35.1 3.4 %attend.1 = bf16[4,256,384]{2,1,0:T(8,128)(2,1)} custom-call(s32[4]{0:T(128)S(1)} %copy-done.6, bf16[256,384]{1,0:T(8,128)(2,1)S(1)} %query.1.query_ref, bf16[256,768]{1,0:T(8,128)(2,1)S(1)} %collective-permute-done.before_ref, bf16[256,768]{1,0:T(8,128)(2,1)S(1)} %get-tuple-element.8.own_ref, bf16[256,768]{1,0:T(8,128)(2,1)S(1)} %collective-permute-done.1.after_ref, ...), custom_call_target="tpu_custom_call" | custom-call | flops 1000000000 | bytes 4000000 | tf_op jit(solution)/shard_map/attend/pallas_call | solution.py:235
  38.6 0.0 copy-start.8
  38.6 4.6 %all-to-all-start = ((bf16[4,256,384]{2,1,0:T(8,128)(2,1)}), bf16[4,256,384]{2,1,0:T(8,128)(2,1)}, u32[]{:S(2)}, u32[]{:S(2)}) async-start(bf16[4,256,384]{2,1,0:T(8,128)(2,1)} %attend.1), calls=%async_computation | async-start | bytes 1572864 | tf_op jit(solution)/shard_map/all_to_all | solution.py:244
  43.2 0.0 copy-done.8
  43.2 0.0 copy-start.3
  43.2 2.0 %copy.12 = bf16[1536,2,384]{2,0,1:T(8,128)(2,1)S(1)} copy(bf16[1536,2,384]{2,1,0:T(2,128)(2,1)} %param.15) | data formatting | bytes 4718592 | tf_op args[6]
  45.2 8.9 %all-to-all-done = bf16[4,256,384]{2,1,0:T(8,128)(2,1)} async-done(((bf16[4,256,384]{2,1,0:T(8,128)(2,1)}), bf16[4,256,384]{2,1,0:T(8,128)(2,1)}, u32[]{:S(2)}, u32[]{:S(2)}) %all-to-all-start) | async-done | bytes 786464 | tf_op jit(solution)/shard_map/all_to_all | solution.py:244
  54.1 1.3 %convert_reduce_fusion.1 = f32[256,384]{1,0:T(8,128)S(1)} fusion(bf16[4,256,384]{2,1,0:T(8,128)(2,1)} %all-to-all-done), kind=kLoop, calls=%fused_computation.2 | loop fusion | flops 688128 | bytes 1179648 | tf_op jit(solution)/shard_map/reduce_sum | solution.py:246
  55.4 0.0 copy-done.3
  55.4 0.1 fusion
  55.5 13.3 %all-gather = bf16[1024,384]{1,0:T(8,128)(2,1)S(1)} all-gather(bf16[256,384]{1,0:T(8,128)(2,1)S(1)} %fusion), channel_id=2, replica_groups=mesh['seq'=128,'tp'=4,'dp'=2] {'tp'}, dimensions={0}, use_global_device_ids=true | all-gather | bytes 983040 | tf_op jit(solution)/shard_map/all_gather | solution.py:247
  68.8 0.0 copy-start.4
  68.8 0.0 copy-start.5
  68.8 1.5 %glu.1.own_ref = bf16[256,384]{1,0:T(8,128)(2,1)S(1)} custom-call(bf16[4,256,384]{2,1,0:T(8,128)(2,1)S(1)} %bitcast.8, f32[1,1536]{1,0:T(1,128)S(1)} %broadcast_in_dim.7.gain_ref, bf16[2,1536,384]{2,1,0:T(8,128)(2,1)S(1)} %bitcast.7), custom_call_target="tpu_custom_call" | custom-call | flops 603979776 | bytes 3500000 | tf_op jit(solution)/shard_map/glu/pallas_call | solution.py:248
  70.3 1.9 %collective-permute-start.3 = (bf16[16,384]{1,0:T(8,128)(2,1)S(1)}, bf16[16,384]{1,0:T(8,128)(2,1)S(1)}, u32[]{:S(2)}, u32[]{:S(2)}) collective-permute-start(bf16[16,384]{1,0:T(8,128)(2,1)S(1)} %get-tuple-element.9), channel_id=1, source_target_pairs={{1,0},{8,1},{9,8},{16,9},{17,16},{24,17},{25,24},{32,25},{33,32},{... | collective-permute-start | bytes 36872 | tf_op jit(solution)/shard_map/ppermute | solution.py:32
  72.3 2.4 %collective-permute-start.2 = (bf16[16,384]{1,0:T(8,128)(2,1)S(1)}, bf16[16,384]{1,0:T(8,128)(2,1)S(1)}, u32[]{:S(2)}, u32[]{:S(2)}) collective-permute-start(bf16[16,384]{1,0:T(8,128)(2,1)S(1)} %get-tuple-element.10), channel_id=1, source_target_pairs={{0,1},{1,8},{8,9},{9,16},{16,17},{17,24},{24,25},{25,32},{32,33},{... | collective-permute-start | bytes 36872 | tf_op jit(solution)/shard_map/ppermute | solution.py:32
  74.7 0.0 collective-permute-done.3.after_ref
  74.7 4.7 %collective-permute-done.2.before_ref = bf16[16,384]{1,0:T(8,128)(2,1)S(1)} collective-permute-done((bf16[16,384]{1,0:T(8,128)(2,1)S(1)}, bf16[16,384]{1,0:T(8,128)(2,1)S(1)}, u32[]{:S(2)}, u32[]{:S(2)}) %collective-permute-start.2) | collective-permute-done | bytes 12320 | tf_op jit(solution)/shard_map/ppermute | solution.py:32
  79.4 0.0 copy-done.4
  79.4 0.0 copy-done.5
  79.4 3.9 %conv.1 = bf16[4,256,384]{2,1,0:T(8,128)(2,1)S(1)} custom-call(s32[4]{0:T(128)S(1)} %copy-done.6, bf16[16,384]{1,0:T(8,128)(2,1)S(1)} %collective-permute-done.2.before_ref, bf16[256,384]{1,0:T(8,128)(2,1)S(1)} %glu.1.own_ref, bf16[16,384]{1,0:T(8,128)(2,1)S(1)} %collective-permute-done.3.after_ref, f32[31,384]{1,0:T(8,128)S(1)} %copy-done.5, ...), custom_call_target="tpu_custom_call" | custom-call | flops 301989888 | bytes 2500000 | tf_op jit(solution)/shard_map/conv/pallas_call | solution.py:259
  83.3 12.4 %all_to_all.10 = bf16[4,256,384]{2,1,0:T(8,128)(2,1)S(1)} all-to-all(bf16[4,256,384]{2,1,0:T(8,128)(2,1)S(1)} %conv.1), channel_id=1, replica_groups=mesh['seq'=128,'tp'=4,'dp'=2] {'tp'}, dimensions={0} | all-to-all | bytes 1572864 | tf_op jit(solution)/shard_map/all_to_all | solution.py:269
  95.7 0.1 convert_reduce_fusion
  95.8 0.8 add_convert_fusion
  (2 shorter events, 0.0 us)
Async XLA Ops:
  0.7 2.0 %copy-start = (bf16[1536,3,384]{2,0,1:T(8,128)(2,1)S(1)}, bf16[1536,3,384]{2,0,1:T(8,128)(2,1)}, u32[]{:S(2)}) copy-start(bf16[1536,3,384]{2,0,1:T(8,128)(2,1)} %param.12) | copy-start | bytes 10616836
  2.7 1.1 %copy-start.2 = (bf16[256,1536]{1,0:T(8,128)(2,1)S(1)}, bf16[256,1536]{1,0:T(8,128)(2,1)}, u32[]{:S(2)}) copy-start(bf16[256,1536]{1,0:T(8,128)(2,1)} %frames_ref.1) | copy-start | bytes 2359300
  3.8 22.0 %copy-start.1 = (bf16[1536,3,384]{2,0,1:T(8,128)(2,1)S(1)}, bf16[1536,3,384]{2,0,1:T(8,128)(2,1)}, u32[]{:S(2)}) copy-start(bf16[1536,3,384]{2,0,1:T(8,128)(2,1)} %param.12) | copy-start | bytes 10616836
  5.5 23.7 %collective-permute-start.1 = (bf16[256,768]{1,0:T(8,128)(2,1)S(1)}, bf16[256,768]{1,0:T(8,128)(2,1)S(1)}, u32[]{:S(2)}, u32[]{:S(2)}) collective-permute-start(bf16[256,768]{1,0:T(8,128)(2,1)S(1)} %get-tuple-element.8.own_ref), channel_id=1, source_target_pairs={{1,0},{8,1},{9,8},{16,9},{17,16},{24,17},{25,24},{32,25},{33,32},{... | collective-permute-start | bytes 1179656 | tf_op jit(solution)/shard_map/ppermute | solution.py:32
  23.9 11.2 %collective-permute-start = (bf16[256,768]{1,0:T(8,128)(2,1)S(1)}, bf16[256,768]{1,0:T(8,128)(2,1)S(1)}, u32[]{:S(2)}, u32[]{:S(2)}) collective-permute-start(bf16[256,768]{1,0:T(8,128)(2,1)S(1)} %get-tuple-element.8.own_ref), channel_id=1, source_target_pairs={{0,1},{1,8},{8,9},{9,16},{16,17},{17,24},{24,25},{25,32},{32,33},{... | collective-permute-start | bytes 1179656 | tf_op jit(solution)/shard_map/ppermute | solution.py:32
  25.9 9.3 %copy-start.6 = (s32[4]{0:T(128)S(1)}, s32[4]{0:T(128)}, u32[]{:S(2)}) copy-start(s32[4]{0:T(128)} %lengths_ref.3) | copy-start | bytes 52
  25.9 9.3 %copy-start.7 = (bf16[384,1536]{1,0:T(8,128)(2,1)S(1)}, bf16[384,1536]{1,0:T(8,128)(2,1)}, u32[]{:S(2)}) copy-start(bf16[384,1536]{1,0:T(8,128)(2,1)} %weight_ref.2) | copy-start | bytes 3538948
  38.6 4.6 %copy-start.8 = (f32[1536]{0:T(1024)S(1)}, f32[1536]{0:T(1024)}, u32[]{:S(2)}) copy-start(f32[1536]{0:T(1024)} %param.14) | copy-start | bytes 18436
  38.6 15.5 %all-to-all-start = ((bf16[4,256,384]{2,1,0:T(8,128)(2,1)}), bf16[4,256,384]{2,1,0:T(8,128)(2,1)}, u32[]{:S(2)}, u32[]{:S(2)}) async-start(bf16[4,256,384]{2,1,0:T(8,128)(2,1)} %attend.1), calls=%async_computation | async-start | bytes 1572864 | tf_op jit(solution)/shard_map/all_to_all | solution.py:244
  43.2 12.2 %copy-start.3 = (bf16[256,1536]{1,0:T(8,128)(2,1)S(1)}, bf16[256,1536]{1,0:T(8,128)(2,1)}, u32[]{:S(2)}) copy-start(bf16[256,1536]{1,0:T(8,128)(2,1)} %frames_ref.1) | copy-start | bytes 2359300
  68.8 10.6 %copy-start.4 = (bf16[384,1536]{1,0:T(8,128)(2,1)S(1)}, bf16[384,1536]{1,0:T(8,128)(2,1)}, u32[]{:S(2)}) copy-start(bf16[384,1536]{1,0:T(8,128)(2,1)} %weight_ref.3) | copy-start | bytes 3538948
  68.8 10.6 %copy-start.5 = (f32[31,384]{1,0:T(8,128)S(1)}, f32[31,384]{1,0:T(8,128)}, u32[]{:S(2)}) copy-start(f32[31,384]{1,0:T(8,128)} %taps_ref.1) | copy-start | bytes 142852
  70.3 4.3 %collective-permute-start.3 = (bf16[16,384]{1,0:T(8,128)(2,1)S(1)}, bf16[16,384]{1,0:T(8,128)(2,1)S(1)}, u32[]{:S(2)}, u32[]{:S(2)}) collective-permute-start(bf16[16,384]{1,0:T(8,128)(2,1)S(1)} %get-tuple-element.9), channel_id=1, source_target_pairs={{1,0},{8,1},{9,8},{16,9},{17,16},{24,17},{25,24},{32,25},{33,32},{... | collective-permute-start | bytes 36872 | tf_op jit(solution)/shard_map/ppermute | solution.py:32
  72.3 7.1 %collective-permute-start.2 = (bf16[16,384]{1,0:T(8,128)(2,1)S(1)}, bf16[16,384]{1,0:T(8,128)(2,1)S(1)}, u32[]{:S(2)}, u32[]{:S(2)}) collective-permute-start(bf16[16,384]{1,0:T(8,128)(2,1)S(1)} %get-tuple-element.10), channel_id=1, source_target_pairs={{0,1},{1,8},{8,9},{9,16},{16,17},{17,24},{24,25},{25,32},{32,33},{... | collective-permute-start | bytes 36872 | tf_op jit(solution)/shard_map/ppermute | solution.py:32

commit v2 on v1

v2 whole, which is shorter than its diff:
```python
import jax
import jax.numpy as jnp
from jax import lax
from jax.experimental import pallas as pl
from jax.experimental.pallas import tpu as pltpu
from jax.sharding import PartitionSpec as P

HEAD = 96
KERNEL = 31
MARGIN = KERNEL // 2
HALO = 16
LANES = 128
EPSILON = 1e-05
LOG2E = 1.4426950408889634
MASKED = -1e38

VMEM = pl.BlockSpec(memory_space=pltpu.VMEM)
HBM = pl.BlockSpec(memory_space=pltpu.HBM)
SMEM = pl.BlockSpec(memory_space=pltpu.SMEM)


def params(mebibytes=48):
    return pltpu.CompilerParams(vmem_limit_bytes=mebibytes * 1024 * 1024)


def cost(flops, size, transcendentals=0):
    return pl.CostEstimate(flops=flops, bytes_accessed=size, transcendentals=transcendentals)


def swap_between_chips(x):
    axes = ("seq", "dp")
    pairs = [(i, i + 1) for i in range(1, lax.axis_size(axes) - 1, 2)]
    return lax.ppermute(x, axes, pairs + [(j, i) for i, j in pairs])


def swap_within_chip(x):
    return lax.ppermute(x, "dp", [(0, 1), (1, 0)])


def matmul(left, right):
    return jnp.dot(left, right, preferred_element_type=jnp.float32)


def first_row(rows):
    return (lax.axis_index("seq") * lax.axis_size("dp") + lax.axis_index("dp")) * rows


def ends_of(lengths_ref):
    ends, total = [], jnp.int32(0)
    for i in range(lengths_ref.shape[0]):
        total = total + lengths_ref[i]
        ends.append(total)
    return ends


def ids_of(positions, ends):
    found = jnp.zeros_like(positions)
    for end in ends:
        found = found + (positions >= end).astype(jnp.int32)
    return jnp.where(positions < 0, -1, found)


def project_kernel(frames_hbm, gain_ref, weight_hbm, normed_ref, out_ref, frames_buf, weight_buf, sems):
    rows, model_width = frames_buf.shape
    cols = weight_buf.shape[2]
    half = rows // 2
    copies = []
    for i in range(2):
        span = pl.ds(i * half, half)
        copies.append(pltpu.make_async_copy(frames_hbm.at[span], frames_buf.at[span], sems.at[i]))
    for i in range(2):
        copies.append(pltpu.make_async_copy(weight_hbm.at[i + 1], weight_buf.at[i], sems.at[i + 2]))
    for copy in copies:
        copy.start()
    for i in range(2):
        copies[i].wait()
        span = slice(i * half, (i + 1) * half)
        values = frames_buf[span].astype(jnp.float32)
        centred = values - jnp.mean(values, axis=-1, keepdims=True)
        inverse = lax.rsqrt(jnp.mean(centred * centred, axis=-1, keepdims=True) + EPSILON)
        for j in range(model_width // LANES):
            lanes = slice(j * LANES, (j + 1) * LANES)
            normed_ref[span, lanes] = (centred[:, lanes] * inverse * gain_ref[j : j + 1]).astype(jnp.bfloat16)
    for i in range(2):
        copies[i + 2].wait()
        out_ref[:, i * cols : (i + 1) * cols] = matmul(normed_ref[...], weight_buf[i]).astype(jnp.bfloat16)


def head_window(head):
    low, high = head * HEAD, (head + 1) * HEAD
    left, right = low // LANES * LANES, -(-high // LANES) * LANES
    lane = left + lax.broadcasted_iota(jnp.int32, (1, right - left), 1)
    return left, right, (lane >= low) & (lane < high)


def scores_of(query, side_ref, left, right, same):
    scores = lax.dot_general(
        query, side_ref[:, left:right], (((1,), (1,)), ((), ())), preferred_element_type=jnp.float32
    )
    return jnp.where(same, scores * (HEAD ** (-0.5) * LOG2E), MASKED)


def place(groups, left, right, mine, rows_value):
    for group in range(left // LANES, right // LANES):
        lanes = slice(group * LANES - left, (group + 1) * LANES - left)
        old, new = groups[group], rows_value[:, lanes]
        groups[group] = new if old is None else jnp.where(mine[:, lanes], new, old)


def own_kernel(lengths_ref, normed_ref, weight_hbm, own_ref, query_ref, mixed_ref, top_ref, total_ref, weight_buf, sem):
    copy = pltpu.make_async_copy(weight_hbm.at[0], weight_buf, sem.at[0])
    copy.start()
    rows, cols = query_ref.shape
    heads = cols // HEAD
    start = first_row(rows)
    ends = ends_of(lengths_ref)
    query_ids = ids_of(start + lax.broadcasted_iota(jnp.int32, (rows, 1), 0), ends)
    same = query_ids == ids_of(start + lax.broadcasted_iota(jnp.int32, (1, rows), 1), ends)
    lane = lax.broadcasted_iota(jnp.int32, (rows, LANES), 1)
    tops = totals = jnp.zeros((rows, LANES), jnp.float32)
    copy.wait()
    queries = matmul(normed_ref[...], weight_buf[...]).astype(jnp.bfloat16)
    query_ref[...] = queries
    groups = [None] * (cols // LANES)
    for head in range(heads):
        left, right, mine = head_window(head)
        query = jnp.where(mine, queries[:, left:right], jnp.zeros((), jnp.bfloat16))
        scores = scores_of(query, own_ref, left, right, same)
        top = jnp.max(scores, axis=-1, keepdims=True)
        weights = jnp.exp2(scores - top)
        tops = jnp.where(lane == head, top, tops)
        totals = jnp.where(lane == head, jnp.sum(weights, axis=-1, keepdims=True), totals)
        place(groups, left, right, mine, matmul(weights.astype(jnp.bfloat16), own_ref[:, cols + left : cols + right]))
    for group, value in enumerate(groups):
        mixed_ref[:, group * LANES : (group + 1) * LANES] = value
    top_ref[...] = tops
    total_ref[...] = totals


def attend_kernel(
    lengths_ref, query_ref, mixed_ref, top_ref, total_ref, inner_ref, outer_ref, weight_ref, out_ref
):
    rows, cols = query_ref.shape
    heads = cols // HEAD
    start = first_row(rows)
    ends = ends_of(lengths_ref)
    query_ids = ids_of(start + lax.broadcasted_iota(jnp.int32, (rows, 1), 0), ends)
    outward = 2 * lax.axis_index("dp") - 1
    same = []
    for step in (outward, -outward):
        at = start + step * rows
        same.append(query_ids == ids_of(at + lax.broadcasted_iota(jnp.int32, (1, rows), 1), ends))
    groups = [None] * (cols // LANES)
    for head in range(heads):
        left, right, mine = head_window(head)
        query = jnp.where(mine, query_ref[:, left:right], jnp.zeros((), jnp.bfloat16))
        outer = scores_of(query, outer_ref, left, right, same[0])
        inner = scores_of(query, inner_ref, left, right, same[1])
        old_top = top_ref[:, head : head + 1]
        top = jnp.maximum(old_top, jnp.max(jnp.maximum(outer, inner), axis=-1, keepdims=True))
        outer, inner = jnp.exp2(outer - top), jnp.exp2(inner - top)
        fade = jnp.exp2(old_top - top)
        total = total_ref[:, head : head + 1] * fade + jnp.sum(outer + inner, axis=-1, keepdims=True)
        mixed = mixed_ref[:, left:right] * fade
        mixed = mixed + matmul(outer.astype(jnp.bfloat16), outer_ref[:, cols + left : cols + right])
        mixed = mixed + matmul(inner.astype(jnp.bfloat16), inner_ref[:, cols + left : cols + right])
        place(groups, left, right, mine, mixed * (1.0 / total))
    mixed_rows = jnp.concatenate([x.astype(jnp.bfloat16) for x in groups], axis=1)
    chunks, _, width = out_ref.shape
    for chunk in range(chunks):
        part = matmul(mixed_rows, weight_ref[:, chunk * width : (chunk + 1) * width])
        out_ref[chunk] = part.astype(jnp.bfloat16)


def glu_kernel(residual_ref, gain_ref, weight_ref, out_ref, outer_ref, inner_ref):
    chunks, rows, width = residual_ref.shape
    model_width = chunks * width
    parts = [residual_ref[i].astype(jnp.float32) for i in range(chunks)]
    mean = sum(jnp.sum(x, axis=-1, keepdims=True) for x in parts) / model_width
    parts = [x - mean for x in parts]
    variance = sum(jnp.sum(x * x, axis=-1, keepdims=True) for x in parts) / model_width
    inverse = lax.rsqrt(variance + EPSILON)
    value = gate = None
    for i in range(chunks):
        normed = []
        for j in range(width // LANES):
            at = i * (width // LANES) + j
            lanes = slice(j * LANES, (j + 1) * LANES)
            normed.append((parts[i][:, lanes] * inverse * gain_ref[at : at + 1]).astype(jnp.bfloat16))
        normed = jnp.concatenate(normed, axis=1)
        span = slice(i * width, (i + 1) * width)
        value_term = matmul(normed, weight_ref[0, span])
        gate_term = matmul(normed, weight_ref[1, span])
        value = value_term if value is None else value + value_term
        gate = gate_term if gate is None else gate + gate_term
    gated = (value * jax.nn.sigmoid(gate)).astype(jnp.bfloat16)
    out_ref[...] = gated
    even = lax.axis_index("dp") == 0
    outer_ref[...] = jnp.where(even, gated[:HALO], gated[rows - HALO :])
    inner_ref[...] = jnp.where(even, gated[rows - HALO :], gated[:HALO])


def spans_of(start, count, ends):
    positions = start + lax.broadcasted_iota(jnp.int32, (count, LANES), 0)
    first = jnp.zeros_like(positions)
    last = jnp.zeros_like(positions)
    begin = jnp.int32(0)
    for end in ends:
        inside = (positions >= begin) & (positions < end)
        first = jnp.where(inside, begin - positions, first)
        last = jnp.where(inside, end - 1 - positions, last)
        begin = end
    return first, last


def convolve(window_ref, base, first, last, taps_ref):
    count = first.shape[0]
    cols = taps_ref.shape[1]
    running = [jnp.zeros((count, LANES), jnp.float32)] * (cols // LANES)
    for tap in range(KERNEL):
        offset = tap - MARGIN
        at = base + HALO + offset
        keep = None if offset == 0 else (first <= offset) if offset < 0 else (last >= offset)
        for group in range(cols // LANES):
            lanes = slice(group * LANES, (group + 1) * LANES)
            term = window_ref[at : at + count, lanes] * taps_ref[tap : tap + 1, lanes]
            if keep is not None:
                term = jnp.where(keep, term, 0.0)
            running[group] = running[group] + term
    return jnp.concatenate([(x * jax.nn.sigmoid(x)).astype(jnp.bfloat16) for x in running], axis=1)


def inside_kernel(lengths_ref, own_ref, taps_ref, out_ref, window_ref):
    start = first_row(own_ref.shape[0]) + HALO
    ends = ends_of(lengths_ref)
    window_ref[...] = own_ref[...].astype(jnp.float32)
    step = 2 * HALO
    for row in range(0, out_ref.shape[0], step):
        first, last = spans_of(start + row, step, ends)
        out_ref[row : row + step] = convolve(window_ref, row, first, last, taps_ref)


def conv_kernel(
    lengths_ref, outer_ref, inner_ref, own_ref, inside_ref, taps_ref, weight_ref, out_ref, low_ref, high_ref
):
    rows = own_ref.shape[0]
    start = first_row(rows)
    ends = ends_of(lengths_ref)
    even = lax.axis_index("dp") == 0
    low_ref[:HALO] = jnp.where(even, outer_ref[...], inner_ref[...]).astype(jnp.float32)
    low_ref[HALO:] = own_ref[: 2 * HALO].astype(jnp.float32)
    high_ref[: 2 * HALO] = own_ref[rows - 2 * HALO :].astype(jnp.float32)
    high_ref[2 * HALO :] = jnp.where(even, inner_ref[...], outer_ref[...]).astype(jnp.float32)
    low = convolve(low_ref, 0, *spans_of(start, HALO, ends), taps_ref)
    high = convolve(high_ref, 0, *spans_of(start + rows - HALO, HALO, ends), taps_ref)
    activated = jnp.concatenate([low, inside_ref[...], high], axis=0)
    chunks, _, width = out_ref.shape
    for chunk in range(chunks):
        part = matmul(activated, weight_ref[:, chunk * width : (chunk + 1) * width])
        out_ref[chunk] = part.astype(jnp.bfloat16)


def body(
    frames,
    lengths,
    norm_gain,
    qkv_weight,
    out_weight,
    conv_gain,
    glu_weight,
    conv_taps,
    point_weight,
):
    rows, model_width = frames.shape
    group_cols = qkv_weight.shape[2]
    chan_cols = glu_weight.shape[2]
    parts = lax.axis_size("tp")
    out_cols = model_width // parts
    bf16 = jnp.bfloat16
    qkv = jnp.swapaxes(qkv_weight, 0, 1)

    shape = jax.ShapeDtypeStruct

    normed, keys_values = pl.pallas_call(
        project_kernel,
        in_specs=[HBM, VMEM, HBM],
        out_specs=[VMEM, VMEM],
        out_shape=[shape((rows, model_width), bf16), shape((rows, 2 * group_cols), bf16)],
        scratch_shapes=[
            pltpu.VMEM((rows, model_width), bf16),
            pltpu.VMEM((2, model_width, group_cols), bf16),
            pltpu.SemaphoreType.DMA((4,)),
        ],
        compiler_params=params(53),
        cost_estimate=cost(4 * rows * model_width * group_cols, 4_000_000),
        name="project",
    )(frames, norm_gain.reshape(-1, LANES), qkv)
    inner = swap_within_chip(keys_values)
    outer = swap_between_chips(keys_values)
    query, mixed, top, total = pl.pallas_call(
        own_kernel,
        in_specs=[SMEM, VMEM, HBM, VMEM],
        out_specs=[VMEM] * 4,
        out_shape=[
            shape((rows, group_cols), bf16),
            shape((rows, group_cols), jnp.float32),
            shape((rows, LANES), jnp.float32),
            shape((rows, LANES), jnp.float32),
        ],
        scratch_shapes=[pltpu.VMEM((model_width, group_cols), bf16), pltpu.SemaphoreType.DMA((1,))],
        compiler_params=params(52),
        cost_estimate=cost(10**9, 4_000_000, 4 * rows * rows),
        name="own",
    )(lengths, normed, qkv, keys_values)
    attn_terms = pl.pallas_call(
        attend_kernel,
        in_specs=[SMEM] + [VMEM] * 7,
        out_specs=VMEM,
        out_shape=shape((parts, rows, out_cols), bf16),
        compiler_params=params(),
        cost_estimate=cost(10**9, 4_000_000, 8 * rows * rows),
        name="attend",
    )(lengths, query, mixed, top, total, inner, outer, out_weight)
    attn_terms = lax.all_to_all(attn_terms, "tp", 0, 0, tiled=True)
    own_frames = lax.dynamic_slice_in_dim(frames, lax.axis_index("tp") * out_cols, out_cols, 1)
    residual = own_frames.astype(jnp.float32) + jnp.sum(attn_terms.astype(jnp.float32), axis=0)
    gathered = lax.all_gather(residual.astype(bf16), "tp", axis=0)
    gated, outer_rows, inner_rows = pl.pallas_call(
        glu_kernel,
        in_specs=[VMEM] * 3,
        out_specs=[VMEM] * 3,
        out_shape=[shape((rows, chan_cols), bf16)] + [shape((HALO, chan_cols), bf16)] * 2,
        compiler_params=params(),
        cost_estimate=cost(4 * rows * model_width * chan_cols, 3_500_000),
        name="glu",
    )(gathered, conv_gain.reshape(-1, LANES), jnp.swapaxes(glu_weight, 0, 1))
    outer_rows = swap_between_chips(outer_rows)
    inner_rows = swap_within_chip(inner_rows)
    inside = pl.pallas_call(
        inside_kernel,
        in_specs=[SMEM, VMEM, VMEM],
        out_specs=VMEM,
        out_shape=shape((rows - 2 * HALO, chan_cols), bf16),
        scratch_shapes=[pltpu.VMEM((rows, chan_cols), jnp.float32)],
        compiler_params=params(),
        cost_estimate=cost(10**9, 4_000_000),
        name="inside",
    )(lengths, gated, conv_taps)
    conv_terms = pl.pallas_call(
        conv_kernel,
        in_specs=[SMEM] + [VMEM] * 6,
        out_specs=VMEM,
        out_shape=shape((parts, rows, out_cols), bf16),
        scratch_shapes=[pltpu.VMEM((3 * HALO, chan_cols), jnp.float32)] * 2,
        compiler_params=params(),
        cost_estimate=cost(2 * rows * model_width * chan_cols, 2_500_000),
        name="conv",
    )(lengths, outer_rows, inner_rows, gated, inside, conv_taps, point_weight)
    conv_terms = lax.all_to_all(conv_terms, "tp", 0, 0, tiled=True)
    return (residual + jnp.sum(conv_terms.astype(jnp.float32), axis=0)).astype(bf16)


def solution(mesh):
    return jax.shard_map(
        body,
        mesh=mesh,
        in_specs=(
            P(("seq", "dp"), None),
            P(),
            P(),
            P(None, None, "tp"),
            P("tp", None),
            P(),
            P(None, None, "tp"),
            P(None, "tp"),
            P("tp", None),
        ),
        out_specs=P(("seq", "dp"), "tp"),
        check_vma=False,
    )
```

time: 97.1 us -> 91.9 us (0.946)
  waiting for transfers between devices: 22.2 us -> 11.5 us
  Pallas kernels: 11.1 us -> 16.2 us
  blocking collectives: 25.7 us -> 29.4 us
  local copies, waits for them, and re-layouts: 5.92 us -> 2.69 us
    ppermute x4, waiting for transfers between devices: 13.4 us -> 0.58 us  [the longest x2 0.58 us: swap_between_chips(): return lax.ppermute(x, axes, pairs + [(j, i) for i, j in pairs])]
    pallas_call x5 -> x6, Pallas kernels: 11.1 us -> 16.2 us  [the longest x1 3.8 us: body(): pl.pallas_call(attend_kernel, in_specs=[SMEM] + [VMEM] * 7, out_specs=VME...]
    all_to_all x1, blocking collectives: 12.4 us -> 15.1 us  [body(): conv_terms = lax.all_to_all(conv_terms, 'tp', 0, 0, tiled=True)]
    unnamed x19 -> x13, local copies, waits for them, and re-layouts: 5.21 us -> 2.69 us
    all_to_all x1, waiting for transfers between devices: 8.88 us -> 11 us  [body(): attn_terms = lax.all_to_all(attn_terms, 'tp', 0, 0, tiled=True)]
    reduce_sum x1, other arithmetic: 1.28 us -> 0.11 us  [body(): jnp.sum(attn_terms.astype(jnp.float32), axis=0)]
  transfers between devices with their start and end apart: 5 -> 5, of which waited for: 4 -> 2; matrix products, arithmetic and copies ran while one was open for 2% -> 2% of each run, Pallas kernels for 1% -> 7%
where the time goes in v2:
time: 91.9 us; the launch traced here: 91.4 us
  blocking collectives  29.4 us (32%)
  starting transfers between devices  28.6 us (31%)
  Pallas kernels  16.2 us (18%)
  waiting for transfers between devices  11.5 us (13%)
  other arithmetic  2.88 us (3%)
  local copies, waits for them, and re-layouts  2.69 us (3%)
    ppermute x2, starting transfers between devices, swap_between_chips(): return lax.ppermute(x, axes, pairs + [(j, i) for i, j in pairs])  20.3 us
    all_to_all x1, blocking collectives, body(): conv_terms = lax.all_to_all(conv_terms, 'tp', 0, 0, tiled=True)  15.1 us
    all_gather x1, blocking collectives, body(): gathered = lax.all_gather(residual.astype(bf16), 'tp', axis=0)  14.3 us
    all_to_all x1, waiting for transfers between devices, body(): attn_terms = lax.all_to_all(attn_terms, 'tp', 0, 0, tiled=True)  11 us
    all_to_all x1, starting transfers between devices, body(): attn_terms = lax.all_to_all(attn_terms, 'tp', 0, 0, tiled=True)  4.47 us
    ppermute x2, starting transfers between devices, swap_within_chip(): return lax.ppermute(x, 'dp', [(0, 1), (1, 0)])  3.84 us
    pallas_call x1, Pallas kernels, body(): pl.pallas_call(attend_kernel, in_specs=[SMEM] + [VMEM] * 7, out_specs=VME...  3.8 us
    pallas_call x1, Pallas kernels, body(): pl.pallas_call(own_kernel, in_specs=[SMEM, VMEM, HBM, VMEM], out_specs=[V...  3.62 us
  transfers between devices with their start and end apart: 5, of which 2 were waited for; matrix products, arithmetic and copies ran while one was open for 2% of the time, Pallas kernels for 7%

profile of v2, /device:TPU:6, one launch (start us, length us, event | category | flops | bytes accessed | tf_op | source)
XLA Modules:
  0.0 91.4 jit_solution(12423369279119975600)
XLA Ops:
  0.0 0.0 copy-start.2
  0.0 0.7 copy-done.2
  0.7 0.0 copy-start.4
  0.7 3.1 %project.1 = (bf16[256,1536]{1,0:T(8,128)(2,1)}, bf16[256,768]{1,0:T(8,128)(2,1)S(1)}) custom-call(bf16[256,1536]{1,0:T(8,128)(2,1)} %frames_hbm.1, f32[12,128]{1,0:T(8,128)S(1)} %bitcast.9, bf16[3,1536,384]{2,1,0:T(8,128)(2,1)} %bitcast.11), custom_call_target="tpu_custom_call" | custom-call | flops 603979776 | bytes 4000000 | tf_op jit(solution)/shard_map/project/pallas_call | solution.py:284
  3.8 18.4 %collective-permute-start.1 = (bf16[256,768]{1,0:T(8,128)(2,1)S(1)}, bf16[256,768]{1,0:T(8,128)(2,1)S(1)}, u32[]{:S(2)}, u32[]{:S(2)}) collective-permute-start(bf16[256,768]{1,0:T(8,128)(2,1)S(1)} %get-tuple-element.15.own_ref), channel_id=1, source_target_pairs={{1,8},{9,16},{17,24},{25,32},{33,40},{41,48},{49,56},{57,64},{65,7... | collective-permute-start | bytes 1179656 | tf_op jit(solution)/shard_map/ppermute | solution.py:33
  22.2 1.9 %collective-permute-start = (bf16[256,768]{1,0:T(8,128)(2,1)S(1)}, bf16[256,768]{1,0:T(8,128)(2,1)S(1)}, u32[]{:S(2)}, u32[]{:S(2)}) collective-permute-start(bf16[256,768]{1,0:T(8,128)(2,1)S(1)} %get-tuple-element.15.own_ref), channel_id=1, source_target_pairs={{0,1},{1,0},{2,3},{3,2},{4,5},{5,4},{6,7},{7,6},{8,9},{9,8},{10,11... | collective-permute-start | bytes 1179656 | tf_op jit(solution)/shard_map/ppermute | solution.py:37
  24.1 0.0 copy-done.4
  24.1 0.0 copy-start.5
  24.2 3.6 %own.1 = (bf16[256,384]{1,0:T(8,128)(2,1)S(1)}, f32[256,384]{1,0:T(8,128)S(1)}, f32[256,128]{1,0:T(8,128)S(1)}, f32[256,128]{1,0:T(8,128)S(1)}) custom-call(s32[4]{0:T(128)S(1)} %copy-done.4, bf16[256,1536]{1,0:T(8,128)(2,1)} %get-tuple-element.14.normed_ref, bf16[3,1536,384]{2,1,0:T(8,128)(2,1)} %bitcast.12, bf16[256,768]{1,0:T(8,128)(2,1)S(1)} %get-tuple-element.15.own_ref), custom_call_target="tpu_custom_call" | custom-call | flops 1000000000 | bytes 4000000 | tf_op jit(solution)/shard_map/own/pallas_call | solution.py:300
  27.8 0.0 collective-permute-done.1.outer_ref
  27.8 0.0 collective-permute-done.inner_ref
  27.8 0.0 copy-done.5
  27.8 3.8 %attend.1 = bf16[4,256,384]{2,1,0:T(8,128)(2,1)} custom-call(s32[4]{0:T(128)S(1)} %copy-done.4, bf16[256,384]{1,0:T(8,128)(2,1)S(1)} %get-tuple-element.16.query_ref, f32[256,384]{1,0:T(8,128)S(1)} %get-tuple-element.17.mixed_ref, f32[256,128]{1,0:T(8,128)S(1)} %get-tuple-element.18.top_ref, f32[256,128]{1,0:T(8,128)S(1)} %get-tuple-element.19.total_ref, ...), custom_call_target="tpu_custom_call" | custom-call | flops 1000000000 | bytes 4000000 | tf_op jit(solution)/shard_map/attend/pallas_call | solution.py:315
  31.6 4.5 %all-to-all-start = ((bf16[4,256,384]{2,1,0:T(8,128)(2,1)}), bf16[4,256,384]{2,1,0:T(8,128)(2,1)S(1)}, u32[]{:S(2)}, u32[]{:S(2)}) async-start(bf16[4,256,384]{2,1,0:T(8,128)(2,1)} %attend.1), calls=%async_computation | async-start | bytes 1572864 | tf_op jit(solution)/shard_map/all_to_all | solution.py:324
  36.1 2.0 %copy.12 = bf16[1536,2,384]{2,0,1:T(8,128)(2,1)S(1)} copy(bf16[1536,2,384]{2,1,0:T(2,128)(2,1)} %param.15) | data formatting | bytes 4718592 | tf_op args[6]
  38.1 0.0 copy-start.3
  38.1 11.0 %all-to-all-done = bf16[4,256,384]{2,1,0:T(8,128)(2,1)S(1)} async-done(((bf16[4,256,384]{2,1,0:T(8,128)(2,1)}), bf16[4,256,384]{2,1,0:T(8,128)(2,1)S(1)}, u32[]{:S(2)}, u32[]{:S(2)}) %all-to-all-start) | async-done | bytes 786464 | tf_op jit(solution)/shard_map/all_to_all | solution.py:324
  49.0 0.1 convert_reduce_fusion.1
  49.1 1.0 %fusion = bf16[256,384]{1,0:T(8,128)(2,1)S(1)} fusion(f32[256,384]{1,0:T(8,128)S(1)} %convert_reduce_fusion.1, bf16[256,1536]{1,0:T(8,128)(2,1)} %frames_hbm.1, s32[]{:T(128)S(6)} %select_n.3), kind=kLoop, calls=%fused_computation.5 | loop fusion | flops 294912 | bytes 786436 | tf_op jit(solution)/shard_map/convert_element_type | solution.py:327
  50.1 14.3 %all-gather = bf16[1024,384]{1,0:T(8,128)(2,1)S(1)} all-gather(bf16[256,384]{1,0:T(8,128)(2,1)S(1)} %fusion), channel_id=2, replica_groups=mesh['seq'=128,'tp'=4,'dp'=2] {'tp'}, dimensions={0}, use_global_device_ids=true | all-gather | bytes 983040 | tf_op jit(solution)/shard_map/all_gather | solution.py:327
  64.4 0.0 copy-done.3
  64.4 0.0 copy-start.1
  64.4 1.5 %glu.1 = (bf16[256,384]{1,0:T(8,128)(2,1)S(1)}, bf16[16,384]{1,0:T(8,128)(2,1)S(1)}, bf16[16,384]{1,0:T(8,128)(2,1)S(1)}) custom-call(bf16[4,256,384]{2,1,0:T(8,128)(2,1)S(1)} %bitcast.8, f32[12,128]{1,0:T(8,128)S(1)} %bitcast.10, bf16[2,1536,384]{2,1,0:T(8,128)(2,1)S(1)} %bitcast.7), custom_call_target="tpu_custom_call" | custom-call | flops 603979776 | bytes 3500000 | tf_op jit(solution)/shard_map/glu/pallas_call | solution.py:328
  65.9 1.9 %collective-permute-start.2 = (bf16[16,384]{1,0:T(8,128)(2,1)S(1)}, bf16[16,384]{1,0:T(8,128)(2,1)S(1)}, u32[]{:S(2)}, u32[]{:S(2)}) collective-permute-start(bf16[16,384]{1,0:T(8,128)(2,1)S(1)} %get-tuple-element.20), channel_id=1, source_target_pairs={{1,8},{9,16},{17,24},{25,32},{33,40},{41,48},{49,56},{57,64},{65,7... | collective-permute-start | bytes 36872 | tf_op jit(solution)/shard_map/ppermute | solution.py:33
  67.9 1.9 %collective-permute-start.3 = (bf16[16,384]{1,0:T(8,128)(2,1)S(1)}, bf16[16,384]{1,0:T(8,128)(2,1)S(1)}, u32[]{:S(2)}, u32[]{:S(2)}) collective-permute-start(bf16[16,384]{1,0:T(8,128)(2,1)S(1)} %get-tuple-element.21), channel_id=1, source_target_pairs={{0,1},{1,0},{2,3},{3,2},{4,5},{5,4},{6,7},{7,6},{8,9},{9,8},{10,11... | collective-permute-start | bytes 36872 | tf_op jit(solution)/shard_map/ppermute | solution.py:37
  69.8 0.0 copy-done.1
  69.8 0.0 copy-start
  69.8 2.7 %inside.1.inside_ref = bf16[224,384]{1,0:T(8,128)(2,1)S(1)} custom-call(s32[4]{0:T(128)S(1)} %copy-done.4, bf16[256,384]{1,0:T(8,128)(2,1)S(1)} %get-tuple-element.22.own_ref, f32[31,384]{1,0:T(8,128)S(1)} %copy-done.1), custom_call_target="tpu_custom_call" | custom-call | flops 1000000000 | bytes 4000000 | tf_op jit(solution)/shard_map/inside/pallas_call | solution.py:339
  72.5 0.6 collective-permute-done.2.outer_ref
  73.1 0.0 collective-permute-done.3.inner_ref
  73.1 0.0 copy-done
  73.1 1.5 %conv.1 = bf16[4,256,384]{2,1,0:T(8,128)(2,1)S(1)} custom-call(s32[4]{0:T(128)S(1)} %copy-done.4, bf16[16,384]{1,0:T(8,128)(2,1)S(1)} %collective-permute-done.2.outer_ref, bf16[16,384]{1,0:T(8,128)(2,1)S(1)} %collective-permute-done.3.inner_ref, bf16[256,384]{1,0:T(8,128)(2,1)S(1)} %get-tuple-element.22.own_ref, bf16[224,384]{1,0:T(8,128)(2,1)S(1)} %inside.1.inside_ref, ...), custom_call_target="tpu_custom_call" | custom-call | flops 301989888 | bytes 2500000 | tf_op jit(solution)/shard_map/conv/pallas_call | solution.py:349
  74.6 15.1 %all_to_all.10 = bf16[4,256,384]{2,1,0:T(8,128)(2,1)S(1)} all-to-all(bf16[4,256,384]{2,1,0:T(8,128)(2,1)S(1)} %conv.1), channel_id=1, replica_groups=mesh['seq'=128,'tp'=4,'dp'=2] {'tp'}, dimensions={0} | all-to-all | bytes 1572864 | tf_op jit(solution)/shard_map/all_to_all | solution.py:359
  89.7 0.1 convert_reduce_fusion
  89.8 1.7 %add_convert_fusion = bf16[256,384]{1,0:T(8,128)(2,1)} fusion(f32[256,384]{1,0:T(8,128)S(1)} %convert_reduce_fusion, f32[256,384]{1,0:T(8,128)S(1)} %convert_reduce_fusion.1, bf16[256,1536]{1,0:T(8,128)(2,1)} %frames_hbm.1, s32[]{:T(128)S(6)} %select_n.3), kind=kLoop, calls=%fused_computation.3 | loop fusion | flops 393216 | bytes 1179652 | tf_op jit(solution)/shard_map/convert_element_type | solution.py:360
Async XLA Ops:
  0.0 0.7 copy-start.2
  0.7 23.4 %copy-start.4 = (s32[4]{0:T(128)S(1)}, s32[4]{0:T(128)}, u32[]{:S(2)}) copy-start(s32[4]{0:T(128)} %lengths_ref.7) | copy-start | bytes 52
  3.8 24.0 %collective-permute-start.1 = (bf16[256,768]{1,0:T(8,128)(2,1)S(1)}, bf16[256,768]{1,0:T(8,128)(2,1)S(1)}, u32[]{:S(2)}, u32[]{:S(2)}) collective-permute-start(bf16[256,768]{1,0:T(8,128)(2,1)S(1)} %get-tuple-element.15.own_ref), channel_id=1, source_target_pairs={{1,8},{9,16},{17,24},{25,32},{33,40},{41,48},{49,56},{57,64},{65,7... | collective-permute-start | bytes 1179656 | tf_op jit(solution)/shard_map/ppermute | solution.py:33
  22.2 5.6 %collective-permute-start = (bf16[256,768]{1,0:T(8,128)(2,1)S(1)}, bf16[256,768]{1,0:T(8,128)(2,1)S(1)}, u32[]{:S(2)}, u32[]{:S(2)}) collective-permute-start(bf16[256,768]{1,0:T(8,128)(2,1)S(1)} %get-tuple-element.15.own_ref), channel_id=1, source_target_pairs={{0,1},{1,0},{2,3},{3,2},{4,5},{5,4},{6,7},{7,6},{8,9},{9,8},{10,11... | collective-permute-start | bytes 1179656 | tf_op jit(solution)/shard_map/ppermute | solution.py:37
  24.1 3.7 %copy-start.5 = (bf16[384,1536]{1,0:T(8,128)(2,1)S(1)}, bf16[384,1536]{1,0:T(8,128)(2,1)}, u32[]{:S(2)}) copy-start(bf16[384,1536]{1,0:T(8,128)(2,1)} %weight_ref.2) | copy-start | bytes 3538948
  31.6 17.4 %all-to-all-start = ((bf16[4,256,384]{2,1,0:T(8,128)(2,1)}), bf16[4,256,384]{2,1,0:T(8,128)(2,1)S(1)}, u32[]{:S(2)}, u32[]{:S(2)}) async-start(bf16[4,256,384]{2,1,0:T(8,128)(2,1)} %attend.1), calls=%async_computation | async-start | bytes 1572864 | tf_op jit(solution)/shard_map/all_to_all | solution.py:324
  38.1 26.4 %copy-start.3 = (f32[1536]{0:T(1024)S(1)}, f32[1536]{0:T(1024)}, u32[]{:S(2)}) copy-start(f32[1536]{0:T(1024)} %param.14) | copy-start | bytes 18436
  64.4 5.4 %copy-start.1 = (f32[31,384]{1,0:T(8,128)S(1)}, f32[31,384]{1,0:T(8,128)}, u32[]{:S(2)}) copy-start(f32[31,384]{1,0:T(8,128)} %taps_ref.3) | copy-start | bytes 142852
  65.9 7.1 %collective-permute-start.2 = (bf16[16,384]{1,0:T(8,128)(2,1)S(1)}, bf16[16,384]{1,0:T(8,128)(2,1)S(1)}, u32[]{:S(2)}, u32[]{:S(2)}) collective-permute-start(bf16[16,384]{1,0:T(8,128)(2,1)S(1)} %get-tuple-element.20), channel_id=1, source_target_pairs={{1,8},{9,16},{17,24},{25,32},{33,40},{41,48},{49,56},{57,64},{65,7... | collective-permute-start | bytes 36872 | tf_op jit(solution)/shard_map/ppermute | solution.py:33
  67.9 5.2 %collective-permute-start.3 = (bf16[16,384]{1,0:T(8,128)(2,1)S(1)}, bf16[16,384]{1,0:T(8,128)(2,1)S(1)}, u32[]{:S(2)}, u32[]{:S(2)}) collective-permute-start(bf16[16,384]{1,0:T(8,128)(2,1)S(1)} %get-tuple-element.21), channel_id=1, source_target_pairs={{0,1},{1,0},{2,3},{3,2},{4,5},{5,4},{6,7},{7,6},{8,9},{9,8},{10,11... | collective-permute-start | bytes 36872 | tf_op jit(solution)/shard_map/ppermute | solution.py:37
  69.8 3.3 %copy-start = (bf16[384,1536]{1,0:T(8,128)(2,1)S(1)}, bf16[384,1536]{1,0:T(8,128)(2,1)}, u32[]{:S(2)}) copy-start(bf16[384,1536]{1,0:T(8,128)(2,1)} %weight_ref.3) | copy-start | bytes 3538948

commit v3 on v2

--- a/solution.py
+++ b/solution.py
@@ -1,3 +1,5 @@
+import functools
+
 import jax
 import jax.numpy as jnp
 from jax import lax
@@ -12,7 +14,6 @@
 LANES = 128
 EPSILON = 1e-05
 LOG2E = 1.4426950408889634
-MASKED = -1e38
 
 VMEM = pl.BlockSpec(memory_space=pltpu.VMEM)
 HBM = pl.BlockSpec(memory_space=pltpu.HBM)
@@ -60,7 +61,9 @@
     return jnp.where(positions < 0, -1, found)
 
 
-def project_kernel(frames_hbm, gain_ref, weight_hbm, normed_ref, out_ref, frames_buf, weight_buf, sems):
+def project_kernel(
+    frames_hbm, gain_hbm, weight_hbm, query_ref, out_ref, frames_buf, gain_buf, weight_buf, normed_ref, sems
+):
     rows, model_width = frames_buf.shape
     cols = weight_buf.shape[2]
     half = rows // 2
@@ -68,10 +71,13 @@
     for i in range(2):
         span = pl.ds(i * half, half)
         copies.append(pltpu.make_async_copy(frames_hbm.at[span], frames_buf.at[span], sems.at[i]))
-    for i in range(2):
-        copies.append(pltpu.make_async_copy(weight_hbm.at[i + 1], weight_buf.at[i], sems.at[i + 2]))
+    for i in range(3):
+        copies.append(pltpu.make_async_copy(weight_hbm.at[(i + 1) % 3], weight_buf.at[i], sems.at[i + 2]))
+    gain_copy = pltpu.make_async_copy(gain_hbm, gain_buf, sems.at[5])
+    gain_copy.start()
     for copy in copies:
         copy.start()
+    gain_copy.wait()
     for i in range(2):
         copies[i].wait()
         span = slice(i * half, (i + 1) * half)
@@ -80,10 +86,12 @@
         inverse = lax.rsqrt(jnp.mean(centred * centred, axis=-1, keepdims=True) + EPSILON)
         for j in range(model_width // LANES):
             lanes = slice(j * LANES, (j + 1) * LANES)
-            normed_ref[span, lanes] = (centred[:, lanes] * inverse * gain_ref[j : j + 1]).astype(jnp.bfloat16)
+            normed_ref[span, lanes] = (centred[:, lanes] * inverse * gain_buf[j : j + 1]).astype(jnp.bfloat16)
     for i in range(2):
         copies[i + 2].wait()
         out_ref[:, i * cols : (i + 1) * cols] = matmul(normed_ref[...], weight_buf[i]).astype(jnp.bfloat16)
+    copies[4].wait()
+    query_ref[...] = matmul(normed_ref[...], weight_buf[2]).astype(jnp.bfloat16)
 
 
 def head_window(head):
@@ -93,11 +101,20 @@
     return left, right, (lane >= low) & (lane < high)
 
 
-def scores_of(query, side_ref, left, right, same):
+def weights_of(query_ref, side_ref, left, right, mine, same):
+    query = jnp.where(mine, query_ref[:, left:right], jnp.zeros((), jnp.bfloat16))
     scores = lax.dot_general(
         query, side_ref[:, left:right], (((1,), (1,)), ((), ())), preferred_element_type=jnp.float32
     )
-    return jnp.where(same, scores * (HEAD ** (-0.5) * LOG2E), MASKED)
+    return jnp.where(same, jnp.exp2(scores * (HEAD ** (-0.5) * LOG2E)), 0.0)
+
+
+def same_utterance(lengths_ref, rows, step):
+    start = first_row(rows)
+    ends = ends_of(lengths_ref)
+    query_ids = ids_of(start + lax.broadcasted_iota(jnp.int32, (rows, 1), 0), ends)
+    at = start + step * rows
+    return query_ids == ids_of(at + lax.broadcasted_iota(jnp.int32, (1, rows), 1), ends)
 
 
 def place(groups, left, right, mine, rows_value):
@@ -107,69 +124,54 @@
         groups[group] = new if old is None else jnp.where(mine[:, lanes], new, old)
 
 
-def own_kernel(lengths_ref, normed_ref, weight_hbm, own_ref, query_ref, mixed_ref, top_ref, total_ref, weight_buf, sem):
-    copy = pltpu.make_async_copy(weight_hbm.at[0], weight_buf, sem.at[0])
-    copy.start()
-    rows, cols = query_ref.shape
-    heads = cols // HEAD
-    start = first_row(rows)
-    ends = ends_of(lengths_ref)
-    query_ids = ids_of(start + lax.broadcasted_iota(jnp.int32, (rows, 1), 0), ends)
-    same = query_ids == ids_of(start + lax.broadcasted_iota(jnp.int32, (1, rows), 1), ends)
-    lane = lax.broadcasted_iota(jnp.int32, (rows, LANES), 1)
-    tops = totals = jnp.zeros((rows, LANES), jnp.float32)
-    copy.wait()
-    queries = matmul(normed_ref[...], weight_buf[...]).astype(jnp.bfloat16)
-    query_ref[...] = queries
-    groups = [None] * (cols // LANES)
-    for head in range(heads):
+def weigh_kernel(outward, lengths_ref, query_ref, side_ref, out_ref):
+    same = same_utterance(lengths_ref, query_ref.shape[0], outward * (2 * lax.axis_index("dp") - 1))
+    for head in range(out_ref.shape[0]):
         left, right, mine = head_window(head)
-        query = jnp.where(mine, queries[:, left:right], jnp.zeros((), jnp.bfloat16))
-        scores = scores_of(query, own_ref, left, right, same)
-        top = jnp.max(scores, axis=-1, keepdims=True)
-        weights = jnp.exp2(scores - top)
-        tops = jnp.where(lane == head, top, tops)
-        totals = jnp.where(lane == head, jnp.sum(weights, axis=-1, keepdims=True), totals)
-        place(groups, left, right, mine, matmul(weights.astype(jnp.bfloat16), own_ref[:, cols + left : cols + right]))
-    for group, value in enumerate(groups):
-        mixed_ref[:, group * LANES : (group + 1) * LANES] = value
-    top_ref[...] = tops
-    total_ref[...] = totals
+        out_ref[head] = weights_of(query_ref, side_ref, left, right, mine, same)
 
 
 def attend_kernel(
-    lengths_ref, query_ref, mixed_ref, top_ref, total_ref, inner_ref, outer_ref, weight_ref, out_ref
+    lengths_ref, query_ref, own_weights_ref, outer_ref, own_ref, inner_ref, inner_weights_ref, weight_ref, out_ref
 ):
     rows, cols = query_ref.shape
-    heads = cols // HEAD
-    start = first_row(rows)
-    ends = ends_of(lengths_ref)
-    query_ids = ids_of(start + lax.broadcasted_iota(jnp.int32, (rows, 1), 0), ends)
-    outward = 2 * lax.axis_index("dp") - 1
-    same = []
-    for step in (outward, -outward):
-        at = start + step * rows
-        same.append(query_ids == ids_of(at + lax.broadcasted_iota(jnp.int32, (1, rows), 1), ends))
+    same = same_utterance(lengths_ref, rows, 2 * lax.axis_index("dp") - 1)
+    sides = (own_ref, inner_ref, outer_ref)
     groups = [None] * (cols // LANES)
-    for head in range(heads):
+    for head in range(cols // HEAD):
         left, right, mine = head_window(head)
-        query = jnp.where(mine, query_ref[:, left:right], jnp.zeros((), jnp.bfloat16))
-        outer = scores_of(query, outer_ref, left, right, same[0])
-        inner = scores_of(query, inner_ref, left, right, same[1])
-        old_top = top_ref[:, head : head + 1]
-        top = jnp.maximum(old_top, jnp.max(jnp.maximum(outer, inner), axis=-1, keepdims=True))
-        outer, inner = jnp.exp2(outer - top), jnp.exp2(inner - top)
-        fade = jnp.exp2(old_top - top)
-        total = total_ref[:, head : head + 1] * fade + jnp.sum(outer + inner, axis=-1, keepdims=True)
-        mixed = mixed_ref[:, left:right] * fade
-        mixed = mixed + matmul(outer.astype(jnp.bfloat16), outer_ref[:, cols + left : cols + right])
-        mixed = mixed + matmul(inner.astype(jnp.bfloat16), inner_ref[:, cols + left : cols + right])
-        place(groups, left, right, mine, mixed * (1.0 / total))
+        outer_weights = weights_of(query_ref, outer_ref, left, right, mine, same)
+        weights = (own_weights_ref[head], inner_weights_ref[head], outer_weights)
+        lane_sums = sum(x[:, i : i + LANES] for x in weights for i in range(0, rows, LANES))
+        total = jnp.sum(lane_sums, axis=-1, keepdims=True)
+        shift = jnp.where(total > 1.0, 2.0**-20, 2.0**20)
+        inverse = 1.0 / (total * shift)
+        mixed = None
+        for x, side in zip(weights, sides):
+            probs = (x * inverse * shift).astype(jnp.bfloat16)
+            term = matmul(probs, side[:, cols + left : cols + right])
+            mixed = term if mixed is None else mixed + term
+        place(groups, left, right, mine, mixed)
     mixed_rows = jnp.concatenate([x.astype(jnp.bfloat16) for x in groups], axis=1)
     chunks, _, width = out_ref.shape
     for chunk in range(chunks):
         part = matmul(mixed_rows, weight_ref[:, chunk * width : (chunk + 1) * width])
         out_ref[chunk] = part.astype(jnp.bfloat16)
+
+
+def merge_kernel(terms_ref, frames_ref, residual_ref, rounded_ref):
+    total = frames_ref[...].astype(jnp.float32)
+    for i in range(terms_ref.shape[0]):
+        total = total + terms_ref[i].astype(jnp.float32)
+    residual_ref[...] = total
+    rounded_ref[...] = total.astype(jnp.bfloat16)
+
+
+def finish_kernel(terms_ref, residual_ref, out_ref):
+    total = residual_ref[...]
+    for i in range(terms_ref.shape[0]):
+        total = total + terms_ref[i].astype(jnp.float32)
+    out_ref[...] = total.astype(jnp.bfloat16)
 
 
 def glu_kernel(residual_ref, gain_ref, weight_ref, out_ref, outer_ref, inner_ref):
@@ -213,14 +215,25 @@
     return first, last
 
 
-def convolve(window_ref, base, first, last, taps_ref):
-    count = first.shape[0]
+def crossed(start, count, ends):
+    found = jnp.bool_(False)
+    for end in ends[:-1]:
+        found = found | ((end > start - MARGIN) & (end < start + count + MARGIN))
+    return found
+
+
+def convolve(window_ref, base, count, start, ends, taps_ref):
     cols = taps_ref.shape[1]
+    first = last = None
+    if start is not None:
+        first, last = spans_of(start, count, ends)
     running = [jnp.zeros((count, LANES), jnp.float32)] * (cols // LANES)
     for tap in range(KERNEL):
         offset = tap - MARGIN
         at = base + HALO + offset
-        keep = None if offset == 0 else (first <= offset) if offset < 0 else (last >= offset)
+        keep = None
+        if first is not None and offset:
+            keep = (first <= offset) if offset < 0 else (last >= offset)
         for group in range(cols // LANES):
             lanes = slice(group * LANES, (group + 1) * LANES)
             term = window_ref[at : at + count, lanes] * taps_ref[tap : tap + 1, lanes]
@@ -235,9 +248,17 @@
     ends = ends_of(lengths_ref)
     window_ref[...] = own_ref[...].astype(jnp.float32)
     step = 2 * HALO
-    for row in range(0, out_ref.shape[0], step):
-        first, last = spans_of(start + row, step, ends)
-        out_ref[row : row + step] = convolve(window_ref, row, first, last, taps_ref)
+    mixed = crossed(start, out_ref.shape[0], ends)
+
+    @pl.when(jnp.logical_not(mixed))
+    def _():
+        for row in range(0, out_ref.shape[0], step):
+            out_ref[row : row + step] = convolve(window_ref, row, step, None, ends, taps_ref)
+
+    @pl.when(mixed)
+    def _():
+        for row in range(0, out_ref.shape[0], step):
+            out_ref[row : row + step] = convolve(window_ref, row, step, start + row, ends, taps_ref)
 
 
 def conv_kernel(
@@ -251,8 +272,8 @@
     low_ref[HALO:] = own_ref[: 2 * HALO].astype(jnp.float32)
     high_ref[: 2 * HALO] = own_ref[rows - 2 * HALO :].astype(jnp.float32)
     high_ref[2 * HALO :] = jnp.where(even, inner_ref[...], outer_ref[...]).astype(jnp.float32)
-    low = convolve(low_ref, 0, *spans_of(start, HALO, ends), taps_ref)
-    high = convolve(high_ref, 0, *spans_of(start + rows - HALO, HALO, ends), taps_ref)
+    low = convolve(low_ref, 0, HALO, start, ends, taps_ref)
+    high = convolve(high_ref, 0, HALO, start + rows - HALO, ends, taps_ref)
     activated = jnp.concatenate([low, inside_ref[...], high], axis=0)
     chunks, _, width = out_ref.shape
     for chunk in range(chunks):
@@ -281,50 +302,59 @@
 
     shape = jax.ShapeDtypeStruct
 
-    normed, keys_values = pl.pallas_call(
+    query, keys_values = pl.pallas_call(
         project_kernel,
-        in_specs=[HBM, VMEM, HBM],
+        in_specs=[HBM, HBM, HBM],
         out_specs=[VMEM, VMEM],
-        out_shape=[shape((rows, model_width), bf16), shape((rows, 2 * group_cols), bf16)],
+        out_shape=[shape((rows, group_cols), bf16), shape((rows, 2 * group_cols), bf16)],
         scratch_shapes=[
             pltpu.VMEM((rows, model_width), bf16),
-            pltpu.VMEM((2, model_width, group_cols), bf16),
-            pltpu.SemaphoreType.DMA((4,)),
+            pltpu.VMEM((model_width // LANES, LANES), jnp.float32),
+            pltpu.VMEM((3, model_width, group_cols), bf16),
+            pltpu.VMEM((rows, model_width), bf16),
+            pltpu.SemaphoreType.DMA((6,)),
         ],
         compiler_params=params(53),
-        cost_estimate=cost(4 * rows * model_width * group_cols, 4_000_000),
+        cost_estimate=cost(6 * rows * model_width * group_cols, 5_000_000),
         name="project",
     )(frames, norm_gain.reshape(-1, LANES), qkv)
     inner = swap_within_chip(keys_values)
     outer = swap_between_chips(keys_values)
-    query, mixed, top, total = pl.pallas_call(
-        own_kernel,
-        in_specs=[SMEM, VMEM, HBM, VMEM],
-        out_specs=[VMEM] * 4,
-        out_shape=[
-            shape((rows, group_cols), bf16),
-            shape((rows, group_cols), jnp.float32),
-            shape((rows, LANES), jnp.float32),
-            shape((rows, LANES), jnp.float32),
-        ],
-        scratch_shapes=[pltpu.VMEM((model_width, group_cols), bf16), pltpu.SemaphoreType.DMA((1,))],
-        compiler_params=params(52),
-        cost_estimate=cost(10**9, 4_000_000, 4 * rows * rows),
-        name="own",
-    )(lengths, normed, qkv, keys_values)
+
+    def weigh(outward, side, name):
+        return pl.pallas_call(
+            functools.partial(weigh_kernel, outward),
+            in_specs=[SMEM, VMEM, VMEM],
+            out_specs=VMEM,
+            out_shape=shape((group_cols // HEAD, rows, rows), jnp.float32),
+            compiler_params=params(40),
+            cost_estimate=cost(1, 1) if outward else cost(10**9, 2_000_000, 4 * rows * rows),
+            name=name,
+        )(lengths, query, side)
+
+    own_weights = weigh(0, keys_values, "weigh_own")
+    inner_weights = weigh(-1, inner, "weigh_inner")
     attn_terms = pl.pallas_call(
         attend_kernel,
         in_specs=[SMEM] + [VMEM] * 7,
         out_specs=VMEM,
         out_shape=shape((parts, rows, out_cols), bf16),
-        compiler_params=params(),
-        cost_estimate=cost(10**9, 4_000_000, 8 * rows * rows),
+        compiler_params=params(40),
+        cost_estimate=cost(10**9, 4_000_000, 4 * rows * rows),
         name="attend",
-    )(lengths, query, mixed, top, total, inner, outer, out_weight)
+    )(lengths, query, own_weights, outer, keys_values, inner, inner_weights, out_weight)
     attn_terms = lax.all_to_all(attn_terms, "tp", 0, 0, tiled=True)
     own_frames = lax.dynamic_slice_in_dim(frames, lax.axis_index("tp") * out_cols, out_cols, 1)
-    residual = own_frames.astype(jnp.float32) + jnp.sum(attn_terms.astype(jnp.float32), axis=0)
-    gathered = lax.all_gather(residual.astype(bf16), "tp", axis=0)
+    residual, rounded = pl.pallas_call(
+        merge_kernel,
+        in_specs=[VMEM] * 2,
+        out_specs=[VMEM] * 2,
+        out_shape=[shape((rows, out_cols), jnp.float32), shape((rows, out_cols), bf16)],
+        compiler_params=params(40),
+        cost_estimate=cost(10**6, 2_000_000),
+        name="merge",
+    )(attn_terms, own_frames)
+    gathered = lax.all_gather(rounded, "tp", axis=0)
     gated, outer_rows, inner_rows = pl.pallas_call(
         glu_kernel,
         in_specs=[VMEM] * 3,
@@ -357,7 +387,15 @@
         name="conv",
     )(lengths, outer_rows, inner_rows, gated, inside, conv_taps, point_weight)
     conv_terms = lax.all_to_all(conv_terms, "tp", 0, 0, tiled=True)
-    return (residual + jnp.sum(conv_terms.astype(jnp.float32), axis=0)).astype(bf16)
+    return pl.pallas_call(
+        finish_kernel,
+        in_specs=[VMEM] * 2,
+        out_specs=VMEM,
+        out_shape=shape((rows, out_cols), bf16),
+        compiler_params=params(40),
+        cost_estimate=cost(10**6, 2_000_000),
+        name="finish",
+    )(conv_terms, residual)
 
 
 def solution(mesh):

time: 91.9 us -> 92.3 us (level)
  starting transfers between devices: 28.6 us -> 34 us
  other arithmetic: 2.88 us -> 0 us
  waiting for transfers between devices: 11.5 us -> 10.2 us
  Pallas kernels: 16.2 us -> 14.9 us
  local copies, waits for them, and re-layouts: 2.69 us -> 3.66 us
    ppermute x2, starting transfers between devices: 20.3 us -> 25.7 us  [swap_between_chips(): return lax.ppermute(x, axes, pairs + [(j, i) for i, j in pairs])]
    all_to_all x1, waiting for transfers between devices: 11 us -> 6.54 us  [body(): attn_terms = lax.all_to_all(attn_terms, 'tp', 0, 0, tiled=True)]
    ppermute x2, waiting for transfers between devices: 0.58 us -> 3.68 us  [swap_between_chips(): return lax.ppermute(x, axes, pairs + [(j, i) for i, j in pairs])]
    convert_element_type x2 -> x0, other arithmetic: 2.66 us -> none  [the longest x1 1.68 us: body(): (residual + jnp.sum(conv_terms.astype(jnp.float32), axis=0)).astype(bf16)]
    all_gather x1, blocking collectives: 14.3 us -> 13.3 us  [body(): gathered = lax.all_gather(rounded, 'tp', axis=0)]
    dynamic_slice x0 -> x1, local copies, waits for them, and re-layouts: none -> 0.95 us  [body(): lax.dynamic_slice_in_dim(frames, lax.axis_index('tp') * out_cols, out_col...]
    pallas_call x2 -> x5, Pallas kernels: 6.73 us -> 6.04 us  [the longest x1 3.38 us: body(): pl.pallas_call(project_kernel, in_specs=[HBM, HBM, HBM], out_specs=[VMEM,...]
  transfers between devices with their start and end apart: 5 -> 5, of which waited for: 2 -> 2; matrix products, arithmetic and copies ran while one was open for 2% -> 3% of each run, Pallas kernels for 7% -> 5%
where the time goes in v3:
time: 92.3 us; the launch traced here: 91.9 us
  starting transfers between devices  34 us (37%)
  blocking collectives  29 us (31%)
  Pallas kernels  14.9 us (16%)
  waiting for transfers between devices  10.2 us (11%)
  local copies, waits for them, and re-layouts  3.66 us (4%)
    ppermute x2, starting transfers between devices, swap_between_chips(): return lax.ppermute(x, axes, pairs + [(j, i) for i, j in pairs])  25.7 us
    all_to_all x1, blocking collectives, body(): conv_terms = lax.all_to_all(conv_terms, 'tp', 0, 0, tiled=True)  15.6 us
    all_gather x1, blocking collectives, body(): gathered = lax.all_gather(rounded, 'tp', axis=0)  13.3 us
    all_to_all x1, waiting for transfers between devices, body(): attn_terms = lax.all_to_all(attn_terms, 'tp', 0, 0, tiled=True)  6.54 us
    all_to_all x1, starting transfers between devices, body(): attn_terms = lax.all_to_all(attn_terms, 'tp', 0, 0, tiled=True)  4.47 us
    ppermute x2, starting transfers between devices, swap_within_chip(): return lax.ppermute(x, 'dp', [(0, 1), (1, 0)])  3.84 us
    ppermute x2, waiting for transfers between devices, swap_between_chips(): return lax.ppermute(x, axes, pairs + [(j, i) for i, j in pairs])  3.68 us
    pallas_call x1, Pallas kernels, body(): pl.pallas_call(project_kernel, in_specs=[HBM, HBM, HBM], out_specs=[VMEM,...  3.38 us
  transfers between devices with their start and end apart: 5, of which 2 were waited for; matrix products, arithmetic and copies ran while one was open for 3% of the time, Pallas kernels for 5%

profile of v3, /device:TPU:6, one launch (start us, length us, event | category | flops | bytes accessed | tf_op | source)
XLA Modules:
  0.0 91.9 jit_solution(11257975711312479801)
XLA Ops:
  0.0 0.0 copy-start.5
  0.0 0.0 copy-start.3
  0.0 0.7 copy-done.3
  0.7 3.4 %project.1 = (bf16[256,384]{1,0:T(8,128)(2,1)S(1)}, bf16[256,768]{1,0:T(8,128)(2,1)S(1)}) custom-call(bf16[256,1536]{1,0:T(8,128)(2,1)} %frames_hbm.1, f32[12,128]{1,0:T(8,128)S(1)} %bitcast.9, bf16[3,1536,384]{2,1,0:T(8,128)(2,1)} %bitcast.11), custom_call_target="tpu_custom_call" | custom-call | flops 905969664 | bytes 5000000 | tf_op jit(solution)/shard_map/project/pallas_call | solution.py:305
  4.1 1.9 %collective-permute-start.1 = (bf16[256,768]{1,0:T(8,128)(2,1)S(1)}, bf16[256,768]{1,0:T(8,128)(2,1)S(1)}, u32[]{:S(2)}, u32[]{:S(2)}) collective-permute-start(bf16[256,768]{1,0:T(8,128)(2,1)S(1)} %get-tuple-element.13.side_ref.own_ref), channel_id=1, source_target_pairs={{0,1},{1,0},{2,3},{3,2},{4,5},{5,4},{6,7},{7,6},{8,9},{9,8},{10,11... | collective-permute-start | bytes 1179656 | tf_op jit(solution)/shard_map/ppermute | solution.py:38
  6.0 19.0 %collective-permute-start = (bf16[256,768]{1,0:T(8,128)(2,1)S(1)}, bf16[256,768]{1,0:T(8,128)(2,1)S(1)}, u32[]{:S(2)}, u32[]{:S(2)}) collective-permute-start(bf16[256,768]{1,0:T(8,128)(2,1)S(1)} %get-tuple-element.13.side_ref.own_ref), channel_id=1, source_target_pairs={{1,8},{9,16},{17,24},{25,32},{33,40},{41,48},{49,56},{57,64},{65,7... | collective-permute-start | bytes 1179656 | tf_op jit(solution)/shard_map/ppermute | solution.py:34
  25.1 0.0 copy-done.5
  25.1 0.0 copy-start.1
  25.1 0.9 weigh_own.1.own_weights_ref
  26.0 0.0 collective-permute-done.1.side_ref.inner_ref
  26.0 0.9 weigh_inner.1.inner_weights_ref
  26.9 3.7 %collective-permute-done.outer_ref = bf16[256,768]{1,0:T(8,128)(2,1)S(1)} collective-permute-done((bf16[256,768]{1,0:T(8,128)(2,1)S(1)}, bf16[256,768]{1,0:T(8,128)(2,1)S(1)}, u32[]{:S(2)}, u32[]{:S(2)}) %collective-permute-start) | collective-permute-done | bytes 393248 | tf_op jit(solution)/shard_map/ppermute | solution.py:34
  30.5 0.0 copy-done.1
  30.5 3.3 %attend.1 = bf16[4,256,384]{2,1,0:T(8,128)(2,1)} custom-call(s32[4]{0:T(128)S(1)} %copy-done.5, bf16[256,384]{1,0:T(8,128)(2,1)S(1)} %get-tuple-element.12.query_ref, f32[4,256,256]{2,1,0:T(8,128)S(1)} %weigh_own.1.own_weights_ref, bf16[256,768]{1,0:T(8,128)(2,1)S(1)} %collective-permute-done.outer_ref, ...), custom_call_target="tpu_custom_call" | custom-call | flops 1000000000 | bytes 4000000 | tf_op jit(solution)/shard_map/attend/pallas_call | solution.py:337
  33.9 4.5 %all-to-all-start = ((bf16[4,256,384]{2,1,0:T(8,128)(2,1)}), bf16[4,256,384]{2,1,0:T(8,128)(2,1)S(1)}, u32[]{:S(2)}, u32[]{:S(2)}) async-start(bf16[4,256,384]{2,1,0:T(8,128)(2,1)} %attend.1), calls=%async_computation | async-start | bytes 1572864 | tf_op jit(solution)/shard_map/all_to_all | solution.py:346
  38.3 2.0 %copy.12 = bf16[1536,2,384]{2,0,1:T(8,128)(2,1)S(1)} copy(bf16[1536,2,384]{2,1,0:T(2,128)(2,1)} %param.15) | data formatting | bytes 4718592 | tf_op args[6]
  40.3 0.0 copy-start.4
  40.3 1.0 %constant_dynamic-slice_fusion.frames_ref = bf16[256,384]{1,0:T(8,128)(2,1)S(1)} fusion(bf16[256,1536]{1,0:T(8,128)(2,1)} %frames_hbm.1, s32[]{:T(128)S(6)} %select_n.3), kind=kLoop, calls=%fused_computation.1 | loop fusion | bytes 393220 | tf_op jit(solution)/shard_map/dynamic_slice | solution.py:347
  41.3 0.0 copy-start.2
  41.3 6.5 %all-to-all-done.terms_ref = bf16[4,256,384]{2,1,0:T(8,128)(2,1)S(1)} async-done(((bf16[4,256,384]{2,1,0:T(8,128)(2,1)}), bf16[4,256,384]{2,1,0:T(8,128)(2,1)S(1)}, u32[]{:S(2)}, u32[]{:S(2)}) %all-to-all-start) | async-done | bytes 786464 | tf_op jit(solution)/shard_map/all_to_all | solution.py:346
  47.8 0.1 merge.1
  48.0 13.3 %all-gather = bf16[1024,384]{1,0:T(8,128)(2,1)S(1)} all-gather(bf16[256,384]{1,0:T(8,128)(2,1)S(1)} %get-tuple-element.14), channel_id=2, replica_groups=mesh['seq'=128,'tp'=4,'dp'=2] {'tp'}, dimensions={0}, use_global_device_ids=true | all-gather | bytes 983040 | tf_op jit(solution)/shard_map/all_gather | solution.py:357
  61.3 0.0 copy-done.4
  61.3 1.5 %glu.1 = (bf16[256,384]{1,0:T(8,128)(2,1)S(1)}, bf16[16,384]{1,0:T(8,128)(2,1)S(1)}, bf16[16,384]{1,0:T(8,128)(2,1)S(1)}) custom-call(bf16[4,256,384]{2,1,0:T(8,128)(2,1)S(1)} %bitcast.8, f32[12,128]{1,0:T(8,128)S(1)} %bitcast.10, bf16[2,1536,384]{2,1,0:T(8,128)(2,1)S(1)} %bitcast.7), custom_call_target="tpu_custom_call" | custom-call | flops 603979776 | bytes 3500000 | tf_op jit(solution)/shard_map/glu/pallas_call | solution.py:358
  62.8 0.0 copy-start
  62.8 6.7 %collective-permute-start.2 = (bf16[16,384]{1,0:T(8,128)(2,1)S(1)}, bf16[16,384]{1,0:T(8,128)(2,1)S(1)}, u32[]{:S(2)}, u32[]{:S(2)}) collective-permute-start(bf16[16,384]{1,0:T(8,128)(2,1)S(1)} %get-tuple-element.15), channel_id=1, source_target_pairs={{1,8},{9,16},{17,24},{25,32},{33,40},{41,48},{49,56},{57,64},{65,7... | collective-permute-start | bytes 36872 | tf_op jit(solution)/shard_map/ppermute | solution.py:34
  69.5 1.9 %collective-permute-start.3 = (bf16[16,384]{1,0:T(8,128)(2,1)S(1)}, bf16[16,384]{1,0:T(8,128)(2,1)S(1)}, u32[]{:S(2)}, u32[]{:S(2)}) collective-permute-start(bf16[16,384]{1,0:T(8,128)(2,1)S(1)} %get-tuple-element.16), channel_id=1, source_target_pairs={{0,1},{1,0},{2,3},{3,2},{4,5},{5,4},{6,7},{7,6},{8,9},{9,8},{10,11... | collective-permute-start | bytes 36872 | tf_op jit(solution)/shard_map/ppermute | solution.py:38
  71.4 0.0 copy-done.2
  71.4 2.6 %inside.1.inside_ref = bf16[224,384]{1,0:T(8,128)(2,1)S(1)} custom-call(s32[4]{0:T(128)S(1)} %copy-done.5, bf16[256,384]{1,0:T(8,128)(2,1)S(1)} %get-tuple-element.17.own_ref, f32[31,384]{1,0:T(8,128)S(1)} %copy-done.2), custom_call_target="tpu_custom_call" | custom-call | flops 1000000000 | bytes 4000000 | tf_op jit(solution)/shard_map/inside/pallas_call | solution.py:369
  74.0 0.0 collective-permute-done.2.outer_ref
  74.0 0.0 collective-permute-done.3.inner_ref
  74.0 0.0 copy-done
  74.0 1.5 %conv.1 = bf16[4,256,384]{2,1,0:T(8,128)(2,1)S(1)} custom-call(s32[4]{0:T(128)S(1)} %copy-done.5, bf16[16,384]{1,0:T(8,128)(2,1)S(1)} %collective-permute-done.2.outer_ref, bf16[16,384]{1,0:T(8,128)(2,1)S(1)} %collective-permute-done.3.inner_ref, bf16[256,384]{1,0:T(8,128)(2,1)S(1)} %get-tuple-element.17.own_ref, bf16[224,384]{1,0:T(8,128)(2,1)S(1)} %inside.1.inside_ref, ...), custom_call_target="tpu_custom_call" | custom-call | flops 301989888 | bytes 2500000 | tf_op jit(solution)/shard_map/conv/pallas_call | solution.py:379
  75.5 15.6 %all_to_all.10.terms_ref = bf16[4,256,384]{2,1,0:T(8,128)(2,1)S(1)} all-to-all(bf16[4,256,384]{2,1,0:T(8,128)(2,1)S(1)} %conv.1), channel_id=1, replica_groups=mesh['seq'=128,'tp'=4,'dp'=2] {'tp'}, dimensions={0} | all-to-all | bytes 1572864 | tf_op jit(solution)/shard_map/all_to_all | solution.py:389
  91.2 0.8 finish.1
Async XLA Ops:
  0.0 25.1 %copy-start.5 = (s32[4]{0:T(128)S(1)}, s32[4]{0:T(128)}, u32[]{:S(2)}) copy-start(s32[4]{0:T(128)} %lengths_ref.9) | copy-start | bytes 52
  0.0 0.7 copy-start.3
  4.1 21.9 %collective-permute-start.1 = (bf16[256,768]{1,0:T(8,128)(2,1)S(1)}, bf16[256,768]{1,0:T(8,128)(2,1)S(1)}, u32[]{:S(2)}, u32[]{:S(2)}) collective-permute-start(bf16[256,768]{1,0:T(8,128)(2,1)S(1)} %get-tuple-element.13.side_ref.own_ref), channel_id=1, source_target_pairs={{0,1},{1,0},{2,3},{3,2},{4,5},{5,4},{6,7},{7,6},{8,9},{9,8},{10,11... | collective-permute-start | bytes 1179656 | tf_op jit(solution)/shard_map/ppermute | solution.py:38
  6.0 24.5 %collective-permute-start = (bf16[256,768]{1,0:T(8,128)(2,1)S(1)}, bf16[256,768]{1,0:T(8,128)(2,1)S(1)}, u32[]{:S(2)}, u32[]{:S(2)}) collective-permute-start(bf16[256,768]{1,0:T(8,128)(2,1)S(1)} %get-tuple-element.13.side_ref.own_ref), channel_id=1, source_target_pairs={{1,8},{9,16},{17,24},{25,32},{33,40},{41,48},{49,56},{57,64},{65,7... | collective-permute-start | bytes 1179656 | tf_op jit(solution)/shard_map/ppermute | solution.py:34
  25.1 5.4 %copy-start.1 = (bf16[384,1536]{1,0:T(8,128)(2,1)S(1)}, bf16[384,1536]{1,0:T(8,128)(2,1)}, u32[]{:S(2)}) copy-start(bf16[384,1536]{1,0:T(8,128)(2,1)} %weight_ref.2) | copy-start | bytes 3538948
  33.9 14.0 %all-to-all-start = ((bf16[4,256,384]{2,1,0:T(8,128)(2,1)}), bf16[4,256,384]{2,1,0:T(8,128)(2,1)S(1)}, u32[]{:S(2)}, u32[]{:S(2)}) async-start(bf16[4,256,384]{2,1,0:T(8,128)(2,1)} %attend.1), calls=%async_computation | async-start | bytes 1572864 | tf_op jit(solution)/shard_map/all_to_all | solution.py:346
  40.3 21.0 %copy-start.4 = (f32[1536]{0:T(1024)S(1)}, f32[1536]{0:T(1024)}, u32[]{:S(2)}) copy-start(f32[1536]{0:T(1024)} %param.14) | copy-start | bytes 18436
  41.3 30.1 %copy-start.2 = (f32[31,384]{1,0:T(8,128)S(1)}, f32[31,384]{1,0:T(8,128)}, u32[]{:S(2)}) copy-start(f32[31,384]{1,0:T(8,128)} %taps_ref.3) | copy-start | bytes 142852
  62.8 11.2 %copy-start = (bf16[384,1536]{1,0:T(8,128)(2,1)S(1)}, bf16[384,1536]{1,0:T(8,128)(2,1)}, u32[]{:S(2)}) copy-start(bf16[384,1536]{1,0:T(8,128)(2,1)} %weight_ref.3) | copy-start | bytes 3538948
  62.8 11.2 %collective-permute-start.2 = (bf16[16,384]{1,0:T(8,128)(2,1)S(1)}, bf16[16,384]{1,0:T(8,128)(2,1)S(1)}, u32[]{:S(2)}, u32[]{:S(2)}) collective-permute-start(bf16[16,384]{1,0:T(8,128)(2,1)S(1)} %get-tuple-element.15), channel_id=1, source_target_pairs={{1,8},{9,16},{17,24},{25,32},{33,40},{41,48},{49,56},{57,64},{65,7... | collective-permute-start | bytes 36872 | tf_op jit(solution)/shard_map/ppermute | solution.py:34
  69.5 4.5 %collective-permute-start.3 = (bf16[16,384]{1,0:T(8,128)(2,1)S(1)}, bf16[16,384]{1,0:T(8,128)(2,1)S(1)}, u32[]{:S(2)}, u32[]{:S(2)}) collective-permute-start(bf16[16,384]{1,0:T(8,128)(2,1)S(1)} %get-tuple-element.16), channel_id=1, source_target_pairs={{0,1},{1,0},{2,3},{3,2},{4,5},{5,4},{6,7},{7,6},{8,9},{9,8},{10,11... | collective-permute-start | bytes 36872 | tf_op jit(solution)/shard_map/ppermute | solution.py:38

commit v4 on v3

--- a/solution.py
+++ b/solution.py
@@ -20,7 +20,7 @@
 SMEM = pl.BlockSpec(memory_space=pltpu.SMEM)
 
 
-def params(mebibytes=48):
+def params(mebibytes=20):
     return pltpu.CompilerParams(vmem_limit_bytes=mebibytes * 1024 * 1024)
 
 
@@ -62,7 +62,7 @@
 
 
 def project_kernel(
-    frames_hbm, gain_hbm, weight_hbm, query_ref, out_ref, frames_buf, gain_buf, weight_buf, normed_ref, sems
+    frames_hbm, gain_hbm, weight_hbm, query_ref, out_ref, edge_ref, frames_buf, gain_buf, weight_buf, normed_ref, sems
 ):
     rows, model_width = frames_buf.shape
     cols = weight_buf.shape[2]
@@ -87,6 +87,8 @@
         for j in range(model_width // LANES):
             lanes = slice(j * LANES, (j + 1) * LANES)
             normed_ref[span, lanes] = (centred[:, lanes] * inverse * gain_buf[j : j + 1]).astype(jnp.bfloat16)
+    edge_ref[:HALO] = frames_buf[:HALO]
+    edge_ref[HALO:] = frames_buf[rows - HALO :]
     for i in range(2):
         copies[i + 2].wait()
         out_ref[:, i * cols : (i + 1) * cols] = matmul(normed_ref[...], weight_buf[i]).astype(jnp.bfloat16)
@@ -132,7 +134,8 @@
 
 
 def attend_kernel(
-    lengths_ref, query_ref, own_weights_ref, outer_ref, own_ref, inner_ref, inner_weights_ref, weight_ref, out_ref
+    lengths_ref, query_ref, own_weights_ref, outer_ref, own_ref, inner_ref, inner_weights_ref, weight_ref, edge_ref,
+    out_ref, outward_ref,
 ):
     rows, cols = query_ref.shape
     same = same_utterance(lengths_ref, rows, 2 * lax.axis_index("dp") - 1)
@@ -153,18 +156,32 @@
             mixed = term if mixed is None else mixed + term
         place(groups, left, right, mine, mixed)
     mixed_rows = jnp.concatenate([x.astype(jnp.bfloat16) for x in groups], axis=1)
+    even = lax.axis_index("dp") == 0
+    outward_ref[:, :cols] = jnp.where(even, mixed_rows[:HALO], mixed_rows[rows - HALO :])
+    outward_ref[:, cols:] = jnp.where(even, edge_ref[:HALO], edge_ref[HALO:])
     chunks, _, width = out_ref.shape
     for chunk in range(chunks):
         part = matmul(mixed_rows, weight_ref[:, chunk * width : (chunk + 1) * width])
         out_ref[chunk] = part.astype(jnp.bfloat16)
 
 
-def merge_kernel(terms_ref, frames_ref, residual_ref, rounded_ref):
+def edge_kernel(outer_ref, weight_ref, out_ref):
+    mixed = outer_ref[:, : weight_ref.shape[0]]
+    chunks, _, width = out_ref.shape
+    for chunk in range(chunks):
+        part = matmul(mixed, weight_ref[:, chunk * width : (chunk + 1) * width])
+        out_ref[chunk] = part.astype(jnp.bfloat16)
+
+
+def merge_kernel(terms_ref, frames_ref, edge_terms_ref, residual_ref, out_ref):
+    rows = frames_ref.shape[0]
     total = frames_ref[...].astype(jnp.float32)
-    for i in range(terms_ref.shape[0]):
+    chunks, edge_rows, _ = edge_terms_ref.shape
+    for i in range(chunks):
         total = total + terms_ref[i].astype(jnp.float32)
+        out_ref[rows + i * edge_rows : rows + (i + 1) * edge_rows] = edge_terms_ref[i]
     residual_ref[...] = total
-    rounded_ref[...] = total.astype(jnp.bfloat16)
+    out_ref[:rows] = total.astype(jnp.bfloat16)
 
 
 def finish_kernel(terms_ref, residual_ref, out_ref):
@@ -174,32 +191,48 @@
     out_ref[...] = total.astype(jnp.bfloat16)
 
 
-def glu_kernel(residual_ref, gain_ref, weight_ref, out_ref, outer_ref, inner_ref):
-    chunks, rows, width = residual_ref.shape
-    model_width = chunks * width
-    parts = [residual_ref[i].astype(jnp.float32) for i in range(chunks)]
+def normalise(parts, gain_ref):
+    model_width = sum(x.shape[1] for x in parts)
     mean = sum(jnp.sum(x, axis=-1, keepdims=True) for x in parts) / model_width
     parts = [x - mean for x in parts]
     variance = sum(jnp.sum(x * x, axis=-1, keepdims=True) for x in parts) / model_width
     inverse = lax.rsqrt(variance + EPSILON)
+    normed, at = [], 0
+    for x in parts:
+        lanes = []
+        for j in range(0, x.shape[1], LANES):
+            lanes.append((x[:, j : j + LANES] * inverse * gain_ref[at : at + 1]).astype(jnp.bfloat16))
+            at += 1
+        normed.append(jnp.concatenate(lanes, axis=1))
+    return normed
+
+
+def glu_kernel(gathered_ref, edge_ref, gain_ref, weight_ref, out_ref, outer_ref, inner_ref):
+    chunks, _, width = gathered_ref.shape
+    rows = out_ref.shape[0]
+    first = edge_ref.shape[1] - chunks * width
+    outer = []
+    for i in range(chunks):
+        at = rows + i * HALO
+        total = edge_ref[:, first + i * width : first + (i + 1) * width].astype(jnp.float32)
+        for j in range(chunks):
+            total = total + gathered_ref[j, at : at + HALO].astype(jnp.float32)
+        outer.append(total)
+    outer = normalise(outer, gain_ref)
+    own = normalise([gathered_ref[i, :rows].astype(jnp.float32) for i in range(chunks)], gain_ref)
     value = gate = None
     for i in range(chunks):
-        normed = []
-        for j in range(width // LANES):
-            at = i * (width // LANES) + j
-            lanes = slice(j * LANES, (j + 1) * LANES)
-            normed.append((parts[i][:, lanes] * inverse * gain_ref[at : at + 1]).astype(jnp.bfloat16))
-        normed = jnp.concatenate(normed, axis=1)
+        normed = jnp.concatenate([own[i], outer[i]], axis=0)
         span = slice(i * width, (i + 1) * width)
         value_term = matmul(normed, weight_ref[0, span])
         gate_term = matmul(normed, weight_ref[1, span])
         value = value_term if value is None else value + value_term
         gate = gate_term if gate is None else gate + gate_term
     gated = (value * jax.nn.sigmoid(gate)).astype(jnp.bfloat16)
-    out_ref[...] = gated
+    out_ref[...] = gated[:rows]
+    outer_ref[...] = gated[rows:]
     even = lax.axis_index("dp") == 0
-    outer_ref[...] = jnp.where(even, gated[:HALO], gated[rows - HALO :])
-    inner_ref[...] = jnp.where(even, gated[rows - HALO :], gated[:HALO])
+    inner_ref[...] = jnp.where(even, gated[rows - HALO : rows], gated[:HALO])
 
 
 def spans_of(start, count, ends):
@@ -222,18 +255,36 @@
     return found
 
 
+def convolve_one(window_ref, taps_ref, sums_ref, out_ref):
+    rows, cols = out_ref.shape
+    count = sums_ref.shape[1]
+    step = 2 * HALO
+    for lane in range(0, cols, LANES):
+        lanes = slice(lane, lane + LANES)
+        for shift in range(8):
+            total = None
+            for at in range(0, KERNEL + 1 - shift, 8):
+                tap = at + shift - 1
+                if tap < 0:
+                    continue
+                term = window_ref[at : at + count, lanes] * taps_ref[tap : tap + 1, lanes]
+                total = term if total is None else total + term
+            sums_ref[shift, :, lanes] = total
+        for row in range(0, rows, step):
+            total = sums_ref[0, row : row + step, lanes]
+            for shift in range(1, 8):
+                total = total + sums_ref[shift, row + shift : row + shift + step, lanes]
+            out_ref[row : row + step, lanes] = (total * jax.nn.sigmoid(total)).astype(jnp.bfloat16)
+
+
 def convolve(window_ref, base, count, start, ends, taps_ref):
     cols = taps_ref.shape[1]
-    first = last = None
-    if start is not None:
-        first, last = spans_of(start, count, ends)
+    first, last = spans_of(start, count, ends)
     running = [jnp.zeros((count, LANES), jnp.float32)] * (cols // LANES)
     for tap in range(KERNEL):
         offset = tap - MARGIN
         at = base + HALO + offset
-        keep = None
-        if first is not None and offset:
-            keep = (first <= offset) if offset < 0 else (last >= offset)
+        keep = None if offset == 0 else (first <= offset) if offset < 0 else (last >= offset)
         for group in range(cols // LANES):
             lanes = slice(group * LANES, (group + 1) * LANES)
             term = window_ref[at : at + count, lanes] * taps_ref[tap : tap + 1, lanes]
@@ -243,7 +294,7 @@
     return jnp.concatenate([(x * jax.nn.sigmoid(x)).astype(jnp.bfloat16) for x in running], axis=1)
 
 
-def inside_kernel(lengths_ref, own_ref, taps_ref, out_ref, window_ref):
+def inside_kernel(lengths_ref, own_ref, taps_ref, out_ref, window_ref, sums_ref):
     start = first_row(own_ref.shape[0]) + HALO
     ends = ends_of(lengths_ref)
     window_ref[...] = own_ref[...].astype(jnp.float32)
@@ -252,8 +303,7 @@
 
     @pl.when(jnp.logical_not(mixed))
     def _():
-        for row in range(0, out_ref.shape[0], step):
-            out_ref[row : row + step] = convolve(window_ref, row, step, None, ends, taps_ref)
+        convolve_one(window_ref, taps_ref, sums_ref, out_ref)
 
     @pl.when(mixed)
     def _():
@@ -302,11 +352,15 @@
 
     shape = jax.ShapeDtypeStruct
 
-    query, keys_values = pl.pallas_call(
+    query, keys_values, edges = pl.pallas_call(
         project_kernel,
         in_specs=[HBM, HBM, HBM],
-        out_specs=[VMEM, VMEM],
-        out_shape=[shape((rows, group_cols), bf16), shape((rows, 2 * group_cols), bf16)],
+        out_specs=[VMEM] * 3,
+        out_shape=[
+            shape((rows, group_cols), bf16),
+            shape((rows, 2 * group_cols), bf16),
+            shape((2 * HALO, model_width), bf16),
+        ],
         scratch_shapes=[
             pltpu.VMEM((rows, model_width), bf16),
             pltpu.VMEM((model_width // LANES, LANES), jnp.float32),
@@ -327,51 +381,64 @@
             in_specs=[SMEM, VMEM, VMEM],
             out_specs=VMEM,
             out_shape=shape((group_cols // HEAD, rows, rows), jnp.float32),
-            compiler_params=params(40),
+            compiler_params=params(16),
             cost_estimate=cost(1, 1) if outward else cost(10**9, 2_000_000, 4 * rows * rows),
             name=name,
         )(lengths, query, side)
 
     own_weights = weigh(0, keys_values, "weigh_own")
     inner_weights = weigh(-1, inner, "weigh_inner")
-    attn_terms = pl.pallas_call(
+    message = shape((HALO, group_cols + model_width), bf16)
+    attn_terms, outward = pl.pallas_call(
         attend_kernel,
-        in_specs=[SMEM] + [VMEM] * 7,
-        out_specs=VMEM,
-        out_shape=shape((parts, rows, out_cols), bf16),
-        compiler_params=params(40),
+        in_specs=[SMEM] + [VMEM] * 8,
+        out_specs=[VMEM] * 2,
+        out_shape=[shape((parts, rows, out_cols), bf16), message],
+        compiler_params=params(16),
         cost_estimate=cost(10**9, 4_000_000, 4 * rows * rows),
         name="attend",
-    )(lengths, query, own_weights, outer, keys_values, inner, inner_weights, out_weight)
+    )(lengths, query, own_weights, outer, keys_values, inner, inner_weights, out_weight, edges)
     attn_terms = lax.all_to_all(attn_terms, "tp", 0, 0, tiled=True)
+    outer_edge = swap_between_chips(outward)
     own_frames = lax.dynamic_slice_in_dim(frames, lax.axis_index("tp") * out_cols, out_cols, 1)
+    edge_terms = pl.pallas_call(
+        edge_kernel,
+        in_specs=[VMEM] * 2,
+        out_specs=VMEM,
+        out_shape=shape((parts, HALO, out_cols), bf16),
+        compiler_params=params(16),
+        cost_estimate=cost(10**8, 2_000_000),
+        name="edge",
+    )(outer_edge, out_weight)
     residual, rounded = pl.pallas_call(
         merge_kernel,
-        in_specs=[VMEM] * 2,
+        in_specs=[VMEM] * 3,
         out_specs=[VMEM] * 2,
-        out_shape=[shape((rows, out_cols), jnp.float32), shape((rows, out_cols), bf16)],
-        compiler_params=params(40),
+        out_shape=[shape((rows, out_cols), jnp.float32), shape((rows + parts * HALO, out_cols), bf16)],
+        compiler_params=params(16),
         cost_estimate=cost(10**6, 2_000_000),
         name="merge",
-    )(attn_terms, own_frames)
+    )(attn_terms, own_frames, edge_terms)
     gathered = lax.all_gather(rounded, "tp", axis=0)
     gated, outer_rows, inner_rows = pl.pallas_call(
         glu_kernel,
-        in_specs=[VMEM] * 3,
+        in_specs=[VMEM] * 4,
         out_specs=[VMEM] * 3,
         out_shape=[shape((rows, chan_cols), bf16)] + [shape((HALO, chan_cols), bf16)] * 2,
         compiler_params=params(),
         cost_estimate=cost(4 * rows * model_width * chan_cols, 3_500_000),
         name="glu",
-    )(gathered, conv_gain.reshape(-1, LANES), jnp.swapaxes(glu_weight, 0, 1))
-    outer_rows = swap_between_chips(outer_rows)
+    )(gathered, outer_edge, conv_gain.reshape(-1, LANES), jnp.swapaxes(glu_weight, 0, 1))
     inner_rows = swap_within_chip(inner_rows)
     inside = pl.pallas_call(
         inside_kernel,
         in_specs=[SMEM, VMEM, VMEM],
         out_specs=VMEM,
         out_shape=shape((rows - 2 * HALO, chan_cols), bf16),
-        scratch_shapes=[pltpu.VMEM((rows, chan_cols), jnp.float32)],
+        scratch_shapes=[
+            pltpu.VMEM((rows, chan_cols), jnp.float32),
+            pltpu.VMEM((8, rows - 3 * HALO // 2, chan_cols), jnp.float32),
+        ],
         compiler_params=params(),
         cost_estimate=cost(10**9, 4_000_000),
         name="inside",
@@ -392,7 +459,7 @@
         in_specs=[VMEM] * 2,
         out_specs=VMEM,
         out_shape=shape((rows, out_cols), bf16),
-        compiler_params=params(40),
+        compiler_params=params(16),
         cost_estimate=cost(10**6, 2_000_000),
         name="finish",
     )(conv_terms, residual)

time: 92.3 us -> 93.7 us (1.015)
  waiting for transfers between devices: 10.2 us -> 4.42 us
  local copies, waits for them, and re-layouts: 3.66 us -> 8.75 us
  blocking collectives: 29 us -> 31.1 us
  starting transfers between devices: 34 us -> 33 us
    all_to_all x1, waiting for transfers between devices: 6.54 us -> 0.01 us  [body(): attn_terms = lax.all_to_all(attn_terms, 'tp', 0, 0, tiled=True)]
    unnamed x13 -> x25, local copies, waits for them, and re-layouts: 2.71 us -> 7.12 us
    pallas_call x4 -> x5, Pallas kernels: 8.36 us -> 10 us  [the longest x1 3.39 us: body(): pl.pallas_call(project_kernel, in_specs=[HBM, HBM, HBM], out_specs=[VMEM]...]
    all_gather x1, blocking collectives: 13.3 us -> 14.7 us  [body(): gathered = lax.all_gather(rounded, 'tp', axis=0)]
    ppermute x2, starting transfers between devices: 25.7 us -> 24.5 us  [swap_between_chips(): return lax.ppermute(x, axes, pairs + [(j, i) for i, j in pairs])]
    pallas_call x1, Pallas kernels: 2.56 us -> 1.62 us  [body(): pl.pallas_call(inside_kernel, in_specs=[SMEM, VMEM, VMEM], out_specs=VMEM...]
  transfers between devices with their start and end apart: 5 -> 5, of which waited for: 2 -> 2; matrix products, arithmetic and copies ran while one was open for 3% -> 4% of each run, Pallas kernels for 5% -> 4%
where the time goes in v4:
time: 93.7 us; the launch traced here: 93 us
  starting transfers between devices  33 us (35%)
  blocking collectives  31.1 us (33%)
  Pallas kernels  15.7 us (17%)
  local copies, waits for them, and re-layouts  8.75 us (9%)
  waiting for transfers between devices  4.42 us (5%)
    ppermute x2, starting transfers between devices, swap_between_chips(): return lax.ppermute(x, axes, pairs + [(j, i) for i, j in pairs])  24.5 us
    all_to_all x1, blocking collectives, body(): conv_terms = lax.all_to_all(conv_terms, 'tp', 0, 0, tiled=True)  16.4 us
    all_gather x1, blocking collectives, body(): gathered = lax.all_gather(rounded, 'tp', axis=0)  14.7 us
    unnamed x25, local copies, waits for them, and re-layouts  7.12 us
    all_to_all x1, starting transfers between devices, body(): attn_terms = lax.all_to_all(attn_terms, 'tp', 0, 0, tiled=True)  4.47 us
    ppermute x2, waiting for transfers between devices, swap_between_chips(): return lax.ppermute(x, axes, pairs + [(j, i) for i, j in pairs])  4.42 us
    ppermute x2, starting transfers between devices, swap_within_chip(): return lax.ppermute(x, 'dp', [(0, 1), (1, 0)])  3.97 us
    pallas_call x1, Pallas kernels, body(): pl.pallas_call(project_kernel, in_specs=[HBM, HBM, HBM], out_specs=[VMEM]...  3.39 us
  transfers between devices with their start and end apart: 5, of which 2 were waited for; matrix products, arithmetic and copies ran while one was open for 4% of the time, Pallas kernels for 4%

profile of v4, /device:TPU:6, one launch (start us, length us, event | category | flops | bytes accessed | tf_op | source)
XLA Modules:
  0.0 93.0 jit_solution(1799587845902845559)
XLA Ops:
  0.0 0.0 copy-start.10
  0.0 0.0 copy-start.8
  0.0 0.7 copy-done.8
  0.7 3.4 %project.1 = (bf16[256,384]{1,0:T(8,128)(2,1)S(1)}, bf16[256,768]{1,0:T(8,128)(2,1)S(1)}, bf16[32,1536]{1,0:T(8,128)(2,1)S(1)}) custom-call(bf16[256,1536]{1,0:T(8,128)(2,1)} %frames_hbm.1, f32[12,128]{1,0:T(8,128)S(1)} %bitcast.9, bf16[3,1536,384]{2,1,0:T(8,128)(2,1)} %bitcast.11), custom_call_target="tpu_custom_call" | custom-call | flops 905969664 | bytes 5000000 | tf_op jit(solution)/shard_map/project/pallas_call | solution.py:355
  4.1 1.9 %collective-permute-start.1 = (bf16[256,768]{1,0:T(8,128)(2,1)S(1)}, bf16[256,768]{1,0:T(8,128)(2,1)S(1)}, u32[]{:S(2)}, u32[]{:S(2)}) collective-permute-start(bf16[256,768]{1,0:T(8,128)(2,1)S(1)} %get-tuple-element.16.side_ref.own_ref), channel_id=1, source_target_pairs={{0,1},{1,0},{2,3},{3,2},{4,5},{5,4},{6,7},{7,6},{8,9},{9,8},{10,11... | collective-permute-start | bytes 1179656 | tf_op jit(solution)/shard_map/ppermute | solution.py:38
  6.0 19.0 %collective-permute-start = (bf16[256,768]{1,0:T(8,128)(2,1)S(1)}, bf16[256,768]{1,0:T(8,128)(2,1)S(1)}, u32[]{:S(2)}, u32[]{:S(2)}) collective-permute-start(bf16[256,768]{1,0:T(8,128)(2,1)S(1)} %get-tuple-element.16.side_ref.own_ref), channel_id=1, source_target_pairs={{1,8},{9,16},{17,24},{25,32},{33,40},{41,48},{49,56},{57,64},{65,7... | collective-permute-start | bytes 1179656 | tf_op jit(solution)/shard_map/ppermute | solution.py:34
  25.1 0.0 copy-done.10
  25.1 0.0 copy-start
  25.1 0.9 weigh_own.1.own_weights_ref
  26.0 0.0 collective-permute-done.1.side_ref.inner_ref
  26.0 0.9 weigh_inner.1.inner_weights_ref
  26.9 3.7 %collective-permute-done.outer_ref = bf16[256,768]{1,0:T(8,128)(2,1)S(1)} collective-permute-done((bf16[256,768]{1,0:T(8,128)(2,1)S(1)}, bf16[256,768]{1,0:T(8,128)(2,1)S(1)}, u32[]{:S(2)}, u32[]{:S(2)}) %collective-permute-start) | collective-permute-done | bytes 393248 | tf_op jit(solution)/shard_map/ppermute | solution.py:34
  30.5 0.0 copy-done
  30.5 3.3 %attend.1 = (bf16[4,256,384]{2,1,0:T(8,128)(2,1)}, bf16[16,1920]{1,0:T(8,128)(2,1)S(1)}) custom-call(s32[4]{0:T(128)S(1)} %copy-done.10, bf16[256,384]{1,0:T(8,128)(2,1)S(1)} %get-tuple-element.15.query_ref, f32[4,256,256]{2,1,0:T(8,128)S(1)} %weigh_own.1.own_weights_ref, bf16[256,768]{1,0:T(8,128)(2,1)S(1)} %collective-permute-done.outer_ref, ...), custom_call_target="tpu_custom_call" | custom-call | flops 1000000000 | bytes 4000000 | tf_op jit(solution)/shard_map/attend/pallas_call | solution.py:392
  33.9 0.0 copy-start.11
  33.9 0.6 copy-done.11
  34.5 4.5 %all-to-all-start = ((bf16[4,256,384]{2,1,0:T(8,128)(2,1)}), bf16[4,256,384]{2,1,0:T(8,128)(2,1)}, u32[]{:S(2)}, u32[]{:S(2)}) async-start(bf16[4,256,384]{2,1,0:T(8,128)(2,1)} %get-tuple-element.18), calls=%async_computation | async-start | bytes 1572864 | tf_op jit(solution)/shard_map/all_to_all | solution.py:401
  39.0 2.0 %copy.12 = bf16[1536,2,384]{2,0,1:T(8,128)(2,1)S(1)} copy(bf16[1536,2,384]{2,1,0:T(2,128)(2,1)} %param.15) | data formatting | bytes 4718592 | tf_op args[6]
  40.9 0.0 copy-start.9
  40.9 5.5 %collective-permute-start.2 = (bf16[16,1920]{1,0:T(8,128)(2,1)}, bf16[16,1920]{1,0:T(8,128)(2,1)S(1)}, u32[]{:S(2)}, u32[]{:S(2)}) collective-permute-start(bf16[16,1920]{1,0:T(8,128)(2,1)} %copy-done.11), channel_id=1, source_target_pairs={{1,8},{9,16},{17,24},{25,32},{33,40},{41,48},{49,56},{57,64},{65,7... | collective-permute-start | bytes 184328 | tf_op jit(solution)/shard_map/ppermute | solution.py:34
  46.4 1.6 %constant_dynamic-slice_fusion.frames_ref = bf16[256,384]{1,0:T(8,128)(2,1)} fusion(bf16[256,1536]{1,0:T(8,128)(2,1)} %frames_hbm.1, s32[]{:T(128)S(6)} %select_n.3), kind=kLoop, calls=%fused_computation.1 | loop fusion | bytes 393220 | tf_op jit(solution)/shard_map/dynamic_slice | solution.py:403
  48.1 0.7 collective-permute-done.2.outer_ref.edge_ref
  48.8 0.3 edge.1.edge_terms_ref
  49.1 0.0 copy-start.3
  49.1 0.6 copy-done.3
  49.7 0.0 copy-start.5
  49.7 0.6 copy-done.5
  50.3 0.0 all-to-all-done.terms_ref
  50.3 0.0 copy-start.2
  50.3 0.9 copy-done.2
  51.3 0.0 copy-start.6
  51.3 0.8 copy-done.6
  52.1 1.3 %merge.1 = (f32[256,384]{1,0:T(8,128)S(1)}, bf16[320,384]{1,0:T(8,128)(2,1)S(1)}) custom-call(bf16[4,256,384]{2,1,0:T(8,128)(2,1)} %all-to-all-done.terms_ref, bf16[256,384]{1,0:T(8,128)(2,1)S(1)} %copy-done.2, bf16[4,16,384]{2,1,0:T(8,128)(2,1)S(1)} %copy-done.6), custom_call_target="tpu_custom_call" | custom-call | flops 1000000 | bytes 2000000 | tf_op jit(solution)/shard_map/merge/pallas_call | solution.py:413
  53.3 0.0 copy-start.7
  53.4 14.7 %all-gather = bf16[1280,384]{1,0:T(8,128)(2,1)S(1)} all-gather(bf16[320,384]{1,0:T(8,128)(2,1)S(1)} %get-tuple-element.20), channel_id=2, replica_groups=mesh['seq'=128,'tp'=4,'dp'=2] {'tp'}, dimensions={0}, use_global_device_ids=true | all-gather | bytes 1228800 | tf_op jit(solution)/shard_map/all_gather | solution.py:422
  68.0 0.0 copy-done.9
  68.1 0.0 copy-start.4
  68.1 0.8 copy-done.4
  68.9 1.7 %glu.1 = (bf16[256,384]{1,0:T(8,128)(2,1)S(1)}, bf16[16,384]{1,0:T(8,128)(2,1)S(1)}, bf16[16,384]{1,0:T(8,128)(2,1)S(1)}) custom-call(bf16[4,320,384]{2,1,0:T(8,128)(2,1)S(1)} %bitcast.8, bf16[16,1920]{1,0:T(8,128)(2,1)S(1)} %copy-done.4, f32[12,128]{1,0:T(8,128)S(1)} %bitcast.10, bf16[2,1536,384]{2,1,0:T(8,128)(2,1)S(1)} %bitcast.7), custom_call_target="tpu_custom_call" | custom-call | flops 603979776 | bytes 3500000 | tf_op jit(solution)/shard_map/glu/pallas_call | solution.py:423
  70.6 0.0 copy-start.1
  70.6 2.1 %collective-permute-start.3 = (bf16[16,384]{1,0:T(8,128)(2,1)S(1)}, bf16[16,384]{1,0:T(8,128)(2,1)S(1)}, u32[]{:S(2)}, u32[]{:S(2)}) collective-permute-start(bf16[16,384]{1,0:T(8,128)(2,1)S(1)} %get-tuple-element.22), channel_id=1, source_target_pairs={{0,1},{1,0},{2,3},{3,2},{4,5},{5,4},{6,7},{7,6},{8,9},{9,8},{10,11... | collective-permute-start | bytes 36872 | tf_op jit(solution)/shard_map/ppermute | solution.py:38
  72.7 0.0 copy-done.7
  72.7 1.6 %inside.1.inside_ref = bf16[224,384]{1,0:T(8,128)(2,1)S(1)} custom-call(s32[4]{0:T(128)S(1)} %copy-done.10, bf16[256,384]{1,0:T(8,128)(2,1)S(1)} %get-tuple-element.23.own_ref, f32[31,384]{1,0:T(8,128)S(1)} %copy-done.7), custom_call_target="tpu_custom_call" | custom-call | flops 1000000000 | bytes 4000000 | tf_op jit(solution)/shard_map/inside/pallas_call | solution.py:433
  74.3 0.0 collective-permute-done.3.inner_ref
  74.4 0.0 copy-done.1
  74.4 1.5 %conv.1 = bf16[4,256,384]{2,1,0:T(8,128)(2,1)S(1)} custom-call(s32[4]{0:T(128)S(1)} %copy-done.10, bf16[16,384]{1,0:T(8,128)(2,1)S(1)} %get-tuple-element.21.outer_ref, bf16[16,384]{1,0:T(8,128)(2,1)S(1)} %collective-permute-done.3.inner_ref, bf16[256,384]{1,0:T(8,128)(2,1)S(1)} %get-tuple-element.23.own_ref, bf16[224,384]{1,0:T(8,128)(2,1)S(1)} %inside.1.inside_ref, ...), custom_call_target="tpu_custom_call" | custom-call | flops 301989888 | bytes 2500000 | tf_op jit(solution)/shard_map/conv/pallas_call | solution.py:446
  75.9 16.4 %all_to_all.10.terms_ref = bf16[4,256,384]{2,1,0:T(8,128)(2,1)S(1)} all-to-all(bf16[4,256,384]{2,1,0:T(8,128)(2,1)S(1)} %conv.1), channel_id=1, replica_groups=mesh['seq'=128,'tp'=4,'dp'=2] {'tp'}, dimensions={0} | all-to-all | bytes 1572864 | tf_op jit(solution)/shard_map/all_to_all | solution.py:456
  92.3 0.8 finish.1
Async XLA Ops:
  0.0 25.1 %copy-start.10 = (s32[4]{0:T(128)S(1)}, s32[4]{0:T(128)}, u32[]{:S(2)}) copy-start(s32[4]{0:T(128)} %lengths_ref.9) | copy-start | bytes 52
  0.0 0.7 copy-start.8
  4.1 21.9 %collective-permute-start.1 = (bf16[256,768]{1,0:T(8,128)(2,1)S(1)}, bf16[256,768]{1,0:T(8,128)(2,1)S(1)}, u32[]{:S(2)}, u32[]{:S(2)}) collective-permute-start(bf16[256,768]{1,0:T(8,128)(2,1)S(1)} %get-tuple-element.16.side_ref.own_ref), channel_id=1, source_target_pairs={{0,1},{1,0},{2,3},{3,2},{4,5},{5,4},{6,7},{7,6},{8,9},{9,8},{10,11... | collective-permute-start | bytes 1179656 | tf_op jit(solution)/shard_map/ppermute | solution.py:38
  6.0 24.5 %collective-permute-start = (bf16[256,768]{1,0:T(8,128)(2,1)S(1)}, bf16[256,768]{1,0:T(8,128)(2,1)S(1)}, u32[]{:S(2)}, u32[]{:S(2)}) collective-permute-start(bf16[256,768]{1,0:T(8,128)(2,1)S(1)} %get-tuple-element.16.side_ref.own_ref), channel_id=1, source_target_pairs={{1,8},{9,16},{17,24},{25,32},{33,40},{41,48},{49,56},{57,64},{65,7... | collective-permute-start | bytes 1179656 | tf_op jit(solution)/shard_map/ppermute | solution.py:34
  25.1 5.4 %copy-start = (bf16[384,1536]{1,0:T(8,128)(2,1)S(1)}, bf16[384,1536]{1,0:T(8,128)(2,1)}, u32[]{:S(2)}) copy-start(bf16[384,1536]{1,0:T(8,128)(2,1)} %weight_ref.4) | copy-start | bytes 3538948
  33.9 0.6 copy-start.11
  34.5 15.8 %all-to-all-start = ((bf16[4,256,384]{2,1,0:T(8,128)(2,1)}), bf16[4,256,384]{2,1,0:T(8,128)(2,1)}, u32[]{:S(2)}, u32[]{:S(2)}) async-start(bf16[4,256,384]{2,1,0:T(8,128)(2,1)} %get-tuple-element.18), calls=%async_computation | async-start | bytes 1572864 | tf_op jit(solution)/shard_map/all_to_all | solution.py:401
  40.9 27.1 %copy-start.9 = (f32[1536]{0:T(1024)S(1)}, f32[1536]{0:T(1024)}, u32[]{:S(2)}) copy-start(f32[1536]{0:T(1024)} %param.14) | copy-start | bytes 18436
  40.9 7.9 %collective-permute-start.2 = (bf16[16,1920]{1,0:T(8,128)(2,1)}, bf16[16,1920]{1,0:T(8,128)(2,1)S(1)}, u32[]{:S(2)}, u32[]{:S(2)}) collective-permute-start(bf16[16,1920]{1,0:T(8,128)(2,1)} %copy-done.11), channel_id=1, source_target_pairs={{1,8},{9,16},{17,24},{25,32},{33,40},{41,48},{49,56},{57,64},{65,7... | collective-permute-start | bytes 184328 | tf_op jit(solution)/shard_map/ppermute | solution.py:34
  49.1 0.6 copy-start.3
  49.7 0.6 copy-start.5
  50.3 0.9 copy-start.2
  51.3 0.8 copy-start.6
  53.3 19.4 %copy-start.7 = (f32[31,384]{1,0:T(8,128)S(1)}, f32[31,384]{1,0:T(8,128)}, u32[]{:S(2)}) copy-start(f32[31,384]{1,0:T(8,128)} %taps_ref.3) | copy-start | bytes 142852
  68.1 0.8 copy-start.4
  70.6 3.7 %copy-start.1 = (bf16[384,1536]{1,0:T(8,128)(2,1)S(1)}, bf16[384,1536]{1,0:T(8,128)(2,1)}, u32[]{:S(2)}) copy-start(bf16[384,1536]{1,0:T(8,128)(2,1)} %weight_ref.5) | copy-start | bytes 3538948
  70.6 3.7 %collective-permute-start.3 = (bf16[16,384]{1,0:T(8,128)(2,1)S(1)}, bf16[16,384]{1,0:T(8,128)(2,1)S(1)}, u32[]{:S(2)}, u32[]{:S(2)}) collective-permute-start(bf16[16,384]{1,0:T(8,128)(2,1)S(1)} %get-tuple-element.22), channel_id=1, source_target_pairs={{0,1},{1,0},{2,3},{3,2},{4,5},{5,4},{6,7},{7,6},{8,9},{9,8},{10,11... | collective-permute-start | bytes 36872 | tf_op jit(solution)/shard_map/ppermute | solution.py:38

commit v5 on v3

--- a/solution.py
+++ b/solution.py
@@ -1,5 +1,3 @@
-import functools
-
 import jax
 import jax.numpy as jnp
 from jax import lax
@@ -20,7 +18,7 @@
 SMEM = pl.BlockSpec(memory_space=pltpu.SMEM)
 
 
-def params(mebibytes=48):
+def params(mebibytes=20):
     return pltpu.CompilerParams(vmem_limit_bytes=mebibytes * 1024 * 1024)
 
 
@@ -124,24 +122,27 @@
         groups[group] = new if old is None else jnp.where(mine[:, lanes], new, old)
 
 
-def weigh_kernel(outward, lengths_ref, query_ref, side_ref, out_ref):
-    same = same_utterance(lengths_ref, query_ref.shape[0], outward * (2 * lax.axis_index("dp") - 1))
+def weigh_kernel(lengths_ref, query_ref, side_ref, out_ref):
+    same = same_utterance(lengths_ref, query_ref.shape[0], 0)
     for head in range(out_ref.shape[0]):
         left, right, mine = head_window(head)
         out_ref[head] = weights_of(query_ref, side_ref, left, right, mine, same)
 
 
 def attend_kernel(
-    lengths_ref, query_ref, own_weights_ref, outer_ref, own_ref, inner_ref, inner_weights_ref, weight_ref, out_ref
+    lengths_ref, query_ref, own_weights_ref, own_ref, inner_ref, outer_ref, weight_ref, out_ref
 ):
     rows, cols = query_ref.shape
-    same = same_utterance(lengths_ref, rows, 2 * lax.axis_index("dp") - 1)
+    outward = 2 * lax.axis_index("dp") - 1
+    same_outer = same_utterance(lengths_ref, rows, outward)
+    same_inner = same_utterance(lengths_ref, rows, -outward)
     sides = (own_ref, inner_ref, outer_ref)
     groups = [None] * (cols // LANES)
     for head in range(cols // HEAD):
         left, right, mine = head_window(head)
-        outer_weights = weights_of(query_ref, outer_ref, left, right, mine, same)
-        weights = (own_weights_ref[head], inner_weights_ref[head], outer_weights)
+        inner_weights = weights_of(query_ref, inner_ref, left, right, mine, same_inner)
+        outer_weights = weights_of(query_ref, outer_ref, left, right, mine, same_outer)
+        weights = (own_weights_ref[head], inner_weights, outer_weights)
         lane_sums = sum(x[:, i : i + LANES] for x in weights for i in range(0, rows, LANES))
         total = jnp.sum(lane_sums, axis=-1, keepdims=True)
         shift = jnp.where(total > 1.0, 2.0**-20, 2.0**20)
@@ -222,18 +223,36 @@
     return found
 
 
+def convolve_one(window_ref, taps_ref, sums_ref, out_ref):
+    rows, cols = out_ref.shape
+    count = sums_ref.shape[1]
+    step = 2 * HALO
+    for lane in range(0, cols, LANES):
+        lanes = slice(lane, lane + LANES)
+        for shift in range(8):
+            total = None
+            for at in range(0, KERNEL + 1 - shift, 8):
+                tap = at + shift - 1
+                if tap < 0:
+                    continue
+                term = window_ref[at : at + count, lanes] * taps_ref[tap : tap + 1, lanes]
+                total = term if total is None else total + term
+            sums_ref[shift, :, lanes] = total
+        for row in range(0, rows, step):
+            total = sums_ref[0, row : row + step, lanes]
+            for shift in range(1, 8):
+                total = total + sums_ref[shift, row + shift : row + shift + step, lanes]
+            out_ref[row : row + step, lanes] = (total * jax.nn.sigmoid(total)).astype(jnp.bfloat16)
+
+
 def convolve(window_ref, base, count, start, ends, taps_ref):
     cols = taps_ref.shape[1]
-    first = last = None
-    if start is not None:
-        first, last = spans_of(start, count, ends)
+    first, last = spans_of(start, count, ends)
     running = [jnp.zeros((count, LANES), jnp.float32)] * (cols // LANES)
     for tap in range(KERNEL):
         offset = tap - MARGIN
         at = base + HALO + offset
-        keep = None
-        if first is not None and offset:
-            keep = (first <= offset) if offset < 0 else (last >= offset)
+        keep = None if offset == 0 else (first <= offset) if offset < 0 else (last >= offset)
         for group in range(cols // LANES):
             lanes = slice(group * LANES, (group + 1) * LANES)
             term = window_ref[at : at + count, lanes] * taps_ref[tap : tap + 1, lanes]
@@ -243,7 +262,7 @@
     return jnp.concatenate([(x * jax.nn.sigmoid(x)).astype(jnp.bfloat16) for x in running], axis=1)
 
 
-def inside_kernel(lengths_ref, own_ref, taps_ref, out_ref, window_ref):
+def inside_kernel(lengths_ref, own_ref, taps_ref, out_ref, window_ref, sums_ref):
     start = first_row(own_ref.shape[0]) + HALO
     ends = ends_of(lengths_ref)
     window_ref[...] = own_ref[...].astype(jnp.float32)
@@ -252,8 +271,7 @@
 
     @pl.when(jnp.logical_not(mixed))
     def _():
-        for row in range(0, out_ref.shape[0], step):
-            out_ref[row : row + step] = convolve(window_ref, row, step, None, ends, taps_ref)
+        convolve_one(window_ref, taps_ref, sums_ref, out_ref)
 
     @pl.when(mixed)
     def _():
@@ -321,28 +339,24 @@
     inner = swap_within_chip(keys_values)
     outer = swap_between_chips(keys_values)
 
-    def weigh(outward, side, name):
-        return pl.pallas_call(
-            functools.partial(weigh_kernel, outward),
-            in_specs=[SMEM, VMEM, VMEM],
-            out_specs=VMEM,
-            out_shape=shape((group_cols // HEAD, rows, rows), jnp.float32),
-            compiler_params=params(40),
-            cost_estimate=cost(1, 1) if outward else cost(10**9, 2_000_000, 4 * rows * rows),
-            name=name,
-        )(lengths, query, side)
-
-    own_weights = weigh(0, keys_values, "weigh_own")
-    inner_weights = weigh(-1, inner, "weigh_inner")
+    own_weights = pl.pallas_call(
+        weigh_kernel,
+        in_specs=[SMEM, VMEM, VMEM],
+        out_specs=VMEM,
+        out_shape=shape((group_cols // HEAD, rows, rows), jnp.float32),
+        compiler_params=params(16),
+        cost_estimate=cost(10**9, 2_000_000, 4 * rows * rows),
+        name="weigh",
+    )(lengths, query, keys_values)
     attn_terms = pl.pallas_call(
         attend_kernel,
-        in_specs=[SMEM] + [VMEM] * 7,
+        in_specs=[SMEM] + [VMEM] * 6,
         out_specs=VMEM,
         out_shape=shape((parts, rows, out_cols), bf16),
-        compiler_params=params(40),
+        compiler_params=params(16),
         cost_estimate=cost(10**9, 4_000_000, 4 * rows * rows),
         name="attend",
-    )(lengths, query, own_weights, outer, keys_values, inner, inner_weights, out_weight)
+    )(lengths, query, own_weights, keys_values, inner, outer, out_weight)
     attn_terms = lax.all_to_all(attn_terms, "tp", 0, 0, tiled=True)
     own_frames = lax.dynamic_slice_in_dim(frames, lax.axis_index("tp") * out_cols, out_cols, 1)
     residual, rounded = pl.pallas_call(
@@ -350,7 +364,7 @@
         in_specs=[VMEM] * 2,
         out_specs=[VMEM] * 2,
         out_shape=[shape((rows, out_cols), jnp.float32), shape((rows, out_cols), bf16)],
-        compiler_params=params(40),
+        compiler_params=params(16),
         cost_estimate=cost(10**6, 2_000_000),
         name="merge",
     )(attn_terms, own_frames)
@@ -371,7 +385,10 @@
         in_specs=[SMEM, VMEM, VMEM],
         out_specs=VMEM,
         out_shape=shape((rows - 2 * HALO, chan_cols), bf16),
-        scratch_shapes=[pltpu.VMEM((rows, chan_cols), jnp.float32)],
+        scratch_shapes=[
+            pltpu.VMEM((rows, chan_cols), jnp.float32),
+            pltpu.VMEM((8, rows - 3 * HALO // 2, chan_cols), jnp.float32),
+        ],
         compiler_params=params(),
         cost_estimate=cost(10**9, 4_000_000),
         name="inside",
@@ -392,7 +409,7 @@
         in_specs=[VMEM] * 2,
         out_specs=VMEM,
         out_shape=shape((rows, out_cols), bf16),
-        compiler_params=params(40),
+        compiler_params=params(16),
         cost_estimate=cost(10**6, 2_000_000),
         name="finish",
     )(conv_terms, residual)

time: 92.3 us -> 88.8 us (0.962)
  starting transfers between devices: 34 us -> 31.7 us
  Pallas kernels: 14.9 us -> 13.3 us
    ppermute x2, starting transfers between devices: 25.7 us -> 23.4 us  [swap_between_chips(): return lax.ppermute(x, axes, pairs + [(j, i) for i, j in pairs])]
    all_to_all x1, waiting for transfers between devices: 6.54 us -> 7.8 us  [body(): attn_terms = lax.all_to_all(attn_terms, 'tp', 0, 0, tiled=True)]
    ppermute x2, waiting for transfers between devices: 3.68 us -> 2.64 us  [swap_between_chips(): return lax.ppermute(x, axes, pairs + [(j, i) for i, j in pairs])]
    pallas_call x1, Pallas kernels: 2.56 us -> 1.62 us  [body(): pl.pallas_call(inside_kernel, in_specs=[SMEM, VMEM, VMEM], out_specs=VMEM...]
    pallas_call x3 -> x2, Pallas kernels: 5.05 us -> 4.34 us  [the longest x1 3.47 us: body(): pl.pallas_call(attend_kernel, in_specs=[SMEM] + [VMEM] * 6, out_specs=VME...]
  transfers between devices with their start and end apart: 5 -> 5, of which waited for: 2 -> 2; matrix products, arithmetic and copies ran while one was open for 3% -> 3% of each run, Pallas kernels for 5% -> 3%
where the time goes in v5:
time: 88.8 us; the launch traced here: 88.4 us
  starting transfers between devices  31.7 us (36%)
  blocking collectives  29.2 us (33%)
  Pallas kernels  13.3 us (15%)
  waiting for transfers between devices  10.4 us (12%)
  local copies, waits for them, and re-layouts  3.66 us (4%)
    ppermute x2, starting transfers between devices, swap_between_chips(): return lax.ppermute(x, axes, pairs + [(j, i) for i, j in pairs])  23.4 us
    all_to_all x1, blocking collectives, body(): conv_terms = lax.all_to_all(conv_terms, 'tp', 0, 0, tiled=True)  15.7 us
    all_gather x1, blocking collectives, body(): gathered = lax.all_gather(rounded, 'tp', axis=0)  13.4 us
    all_to_all x1, waiting for transfers between devices, body(): attn_terms = lax.all_to_all(attn_terms, 'tp', 0, 0, tiled=True)  7.8 us
    all_to_all x1, starting transfers between devices, body(): attn_terms = lax.all_to_all(attn_terms, 'tp', 0, 0, tiled=True)  4.46 us
    ppermute x2, starting transfers between devices, swap_within_chip(): return lax.ppermute(x, 'dp', [(0, 1), (1, 0)])  3.84 us
    pallas_call x1, Pallas kernels, body(): pl.pallas_call(attend_kernel, in_specs=[SMEM] + [VMEM] * 6, out_specs=VME...  3.47 us
    pallas_call x1, Pallas kernels, body(): pl.pallas_call(project_kernel, in_specs=[HBM, HBM, HBM], out_specs=[VMEM,...  3.38 us
  transfers between devices with their start and end apart: 5, of which 2 were waited for; matrix products, arithmetic and copies ran while one was open for 3% of the time, Pallas kernels for 3%

profile of v5, /device:TPU:6, one launch (start us, length us, event | category | flops | bytes accessed | tf_op | source)
XLA Modules:
  0.0 88.4 jit_solution(13867679737809756593)
XLA Ops:
  0.0 0.0 copy-start.5
  0.0 0.0 copy-start.3
  0.0 0.7 copy-done.3
  0.7 3.4 %project.1 = (bf16[256,384]{1,0:T(8,128)(2,1)S(1)}, bf16[256,768]{1,0:T(8,128)(2,1)S(1)}) custom-call(bf16[256,1536]{1,0:T(8,128)(2,1)} %frames_hbm.1, f32[12,128]{1,0:T(8,128)S(1)} %bitcast.9, bf16[3,1536,384]{2,1,0:T(8,128)(2,1)} %bitcast.11), custom_call_target="tpu_custom_call" | custom-call | flops 905969664 | bytes 5000000 | tf_op jit(solution)/shard_map/project/pallas_call | solution.py:323
  4.1 0.0 copy-start
  4.1 18.5 %collective-permute-start.1 = (bf16[256,768]{1,0:T(8,128)(2,1)S(1)}, bf16[256,768]{1,0:T(8,128)(2,1)S(1)}, u32[]{:S(2)}, u32[]{:S(2)}) collective-permute-start(bf16[256,768]{1,0:T(8,128)(2,1)S(1)} %get-tuple-element.13.side_ref.own_ref), channel_id=1, source_target_pairs={{1,8},{9,16},{17,24},{25,32},{33,40},{41,48},{49,56},{57,64},{65,7... | collective-permute-start | bytes 1179656 | tf_op jit(solution)/shard_map/ppermute | solution.py:32
  22.6 1.9 %collective-permute-start = (bf16[256,768]{1,0:T(8,128)(2,1)S(1)}, bf16[256,768]{1,0:T(8,128)(2,1)S(1)}, u32[]{:S(2)}, u32[]{:S(2)}) collective-permute-start(bf16[256,768]{1,0:T(8,128)(2,1)S(1)} %get-tuple-element.13.side_ref.own_ref), channel_id=1, source_target_pairs={{0,1},{1,0},{2,3},{3,2},{4,5},{5,4},{6,7},{7,6},{8,9},{9,8},{10,11... | collective-permute-start | bytes 1179656 | tf_op jit(solution)/shard_map/ppermute | solution.py:36
  24.6 0.0 copy-done.5
  24.6 0.9 weigh.1.own_weights_ref
  25.4 2.6 %collective-permute-done.1.outer_ref = bf16[256,768]{1,0:T(8,128)(2,1)S(1)} collective-permute-done((bf16[256,768]{1,0:T(8,128)(2,1)S(1)}, bf16[256,768]{1,0:T(8,128)(2,1)S(1)}, u32[]{:S(2)}, u32[]{:S(2)}) %collective-permute-start.1) | collective-permute-done | bytes 393248 | tf_op jit(solution)/shard_map/ppermute | solution.py:32
  28.1 0.0 collective-permute-done.inner_ref
  28.1 0.0 copy-done
  28.1 3.5 %attend.1 = bf16[4,256,384]{2,1,0:T(8,128)(2,1)} custom-call(s32[4]{0:T(128)S(1)} %copy-done.5, bf16[256,384]{1,0:T(8,128)(2,1)S(1)} %get-tuple-element.12.query_ref, f32[4,256,256]{2,1,0:T(8,128)S(1)} %weigh.1.own_weights_ref, bf16[256,768]{1,0:T(8,128)(2,1)S(1)} %get-tuple-element.13.side_ref.own_ref, bf16[256,768]{1,0:T(8,128)(2,1)S(1)} %collective-permute-done.inner_ref, ...), custom_call_target="tpu_custom_call" | custom-call | flops 1000000000 | bytes 4000000 | tf_op jit(solution)/shard_map/attend/pallas_call | solution.py:351
  31.6 4.5 %all-to-all-start = ((bf16[4,256,384]{2,1,0:T(8,128)(2,1)}), bf16[4,256,384]{2,1,0:T(8,128)(2,1)S(1)}, u32[]{:S(2)}, u32[]{:S(2)}) async-start(bf16[4,256,384]{2,1,0:T(8,128)(2,1)} %attend.1), calls=%async_computation | async-start | bytes 1572864 | tf_op jit(solution)/shard_map/all_to_all | solution.py:360
  36.0 2.0 %copy.12 = bf16[1536,2,384]{2,0,1:T(8,128)(2,1)S(1)} copy(bf16[1536,2,384]{2,1,0:T(2,128)(2,1)} %param.15) | data formatting | bytes 4718592 | tf_op args[6]
  38.0 0.0 copy-start.4
  38.0 1.0 %constant_dynamic-slice_fusion.frames_ref = bf16[256,384]{1,0:T(8,128)(2,1)S(1)} fusion(bf16[256,1536]{1,0:T(8,128)(2,1)} %frames_hbm.1, s32[]{:T(128)S(6)} %select_n.3), kind=kLoop, calls=%fused_computation.1 | loop fusion | bytes 393220 | tf_op jit(solution)/shard_map/dynamic_slice | solution.py:361
  39.0 0.0 copy-start.2
  39.0 7.8 %all-to-all-done.terms_ref = bf16[4,256,384]{2,1,0:T(8,128)(2,1)S(1)} async-done(((bf16[4,256,384]{2,1,0:T(8,128)(2,1)}), bf16[4,256,384]{2,1,0:T(8,128)(2,1)S(1)}, u32[]{:S(2)}, u32[]{:S(2)}) %all-to-all-start) | async-done | bytes 786464 | tf_op jit(solution)/shard_map/all_to_all | solution.py:360
  46.8 0.1 merge.1
  46.9 13.4 %all-gather = bf16[1024,384]{1,0:T(8,128)(2,1)S(1)} all-gather(bf16[256,384]{1,0:T(8,128)(2,1)S(1)} %get-tuple-element.14), channel_id=2, replica_groups=mesh['seq'=128,'tp'=4,'dp'=2] {'tp'}, dimensions={0}, use_global_device_ids=true | all-gather | bytes 983040 | tf_op jit(solution)/shard_map/all_gather | solution.py:371
  60.4 0.0 copy-done.4
  60.4 1.5 %glu.1 = (bf16[256,384]{1,0:T(8,128)(2,1)S(1)}, bf16[16,384]{1,0:T(8,128)(2,1)S(1)}, bf16[16,384]{1,0:T(8,128)(2,1)S(1)}) custom-call(bf16[4,256,384]{2,1,0:T(8,128)(2,1)S(1)} %bitcast.8, f32[12,128]{1,0:T(8,128)S(1)} %bitcast.10, bf16[2,1536,384]{2,1,0:T(8,128)(2,1)S(1)} %bitcast.7), custom_call_target="tpu_custom_call" | custom-call | flops 603979776 | bytes 3500000 | tf_op jit(solution)/shard_map/glu/pallas_call | solution.py:372
  61.9 0.0 copy-start.1
  61.9 4.9 %collective-permute-start.2 = (bf16[16,384]{1,0:T(8,128)(2,1)S(1)}, bf16[16,384]{1,0:T(8,128)(2,1)S(1)}, u32[]{:S(2)}, u32[]{:S(2)}) collective-permute-start(bf16[16,384]{1,0:T(8,128)(2,1)S(1)} %get-tuple-element.15), channel_id=1, source_target_pairs={{1,8},{9,16},{17,24},{25,32},{33,40},{41,48},{49,56},{57,64},{65,7... | collective-permute-start | bytes 36872 | tf_op jit(solution)/shard_map/ppermute | solution.py:32
  66.8 1.9 %collective-permute-start.3 = (bf16[16,384]{1,0:T(8,128)(2,1)S(1)}, bf16[16,384]{1,0:T(8,128)(2,1)S(1)}, u32[]{:S(2)}, u32[]{:S(2)}) collective-permute-start(bf16[16,384]{1,0:T(8,128)(2,1)S(1)} %get-tuple-element.16), channel_id=1, source_target_pairs={{0,1},{1,0},{2,3},{3,2},{4,5},{5,4},{6,7},{7,6},{8,9},{9,8},{10,11... | collective-permute-start | bytes 36872 | tf_op jit(solution)/shard_map/ppermute | solution.py:36
  68.7 0.0 copy-done.2
  68.7 1.6 %inside.1.inside_ref = bf16[224,384]{1,0:T(8,128)(2,1)S(1)} custom-call(s32[4]{0:T(128)S(1)} %copy-done.5, bf16[256,384]{1,0:T(8,128)(2,1)S(1)} %get-tuple-element.17.own_ref, f32[31,384]{1,0:T(8,128)S(1)} %copy-done.2), custom_call_target="tpu_custom_call" | custom-call | flops 1000000000 | bytes 4000000 | tf_op jit(solution)/shard_map/inside/pallas_call | solution.py:383
  70.4 0.0 collective-permute-done.2.outer_ref
  70.4 0.0 collective-permute-done.3.inner_ref
  70.4 0.0 copy-done.1
  70.4 1.5 %conv.1 = bf16[4,256,384]{2,1,0:T(8,128)(2,1)S(1)} custom-call(s32[4]{0:T(128)S(1)} %copy-done.5, bf16[16,384]{1,0:T(8,128)(2,1)S(1)} %collective-permute-done.2.outer_ref, bf16[16,384]{1,0:T(8,128)(2,1)S(1)} %collective-permute-done.3.inner_ref, bf16[256,384]{1,0:T(8,128)(2,1)S(1)} %get-tuple-element.17.own_ref, bf16[224,384]{1,0:T(8,128)(2,1)S(1)} %inside.1.inside_ref, ...), custom_call_target="tpu_custom_call" | custom-call | flops 301989888 | bytes 2500000 | tf_op jit(solution)/shard_map/conv/pallas_call | solution.py:396
  71.9 15.7 %all_to_all.10.terms_ref = bf16[4,256,384]{2,1,0:T(8,128)(2,1)S(1)} all-to-all(bf16[4,256,384]{2,1,0:T(8,128)(2,1)S(1)} %conv.1), channel_id=1, replica_groups=mesh['seq'=128,'tp'=4,'dp'=2] {'tp'}, dimensions={0} | all-to-all | bytes 1572864 | tf_op jit(solution)/shard_map/all_to_all | solution.py:406
  87.6 0.8 finish.1
Async XLA Ops:
  0.0 24.6 %copy-start.5 = (s32[4]{0:T(128)S(1)}, s32[4]{0:T(128)}, u32[]{:S(2)}) copy-start(s32[4]{0:T(128)} %lengths_ref.7) | copy-start | bytes 52
  0.0 0.7 copy-start.3
  4.1 24.0 %copy-start = (bf16[384,1536]{1,0:T(8,128)(2,1)S(1)}, bf16[384,1536]{1,0:T(8,128)(2,1)}, u32[]{:S(2)}) copy-start(bf16[384,1536]{1,0:T(8,128)(2,1)} %weight_ref.2) | copy-start | bytes 3538948
  4.1 24.0 %collective-permute-start.1 = (bf16[256,768]{1,0:T(8,128)(2,1)S(1)}, bf16[256,768]{1,0:T(8,128)(2,1)S(1)}, u32[]{:S(2)}, u32[]{:S(2)}) collective-permute-start(bf16[256,768]{1,0:T(8,128)(2,1)S(1)} %get-tuple-element.13.side_ref.own_ref), channel_id=1, source_target_pairs={{1,8},{9,16},{17,24},{25,32},{33,40},{41,48},{49,56},{57,64},{65,7... | collective-permute-start | bytes 1179656 | tf_op jit(solution)/shard_map/ppermute | solution.py:32
  22.6 5.4 %collective-permute-start = (bf16[256,768]{1,0:T(8,128)(2,1)S(1)}, bf16[256,768]{1,0:T(8,128)(2,1)S(1)}, u32[]{:S(2)}, u32[]{:S(2)}) collective-permute-start(bf16[256,768]{1,0:T(8,128)(2,1)S(1)} %get-tuple-element.13.side_ref.own_ref), channel_id=1, source_target_pairs={{0,1},{1,0},{2,3},{3,2},{4,5},{5,4},{6,7},{7,6},{8,9},{9,8},{10,11... | collective-permute-start | bytes 1179656 | tf_op jit(solution)/shard_map/ppermute | solution.py:36
  31.6 15.2 %all-to-all-start = ((bf16[4,256,384]{2,1,0:T(8,128)(2,1)}), bf16[4,256,384]{2,1,0:T(8,128)(2,1)S(1)}, u32[]{:S(2)}, u32[]{:S(2)}) async-start(bf16[4,256,384]{2,1,0:T(8,128)(2,1)} %attend.1), calls=%async_computation | async-start | bytes 1572864 | tf_op jit(solution)/shard_map/all_to_all | solution.py:360
  38.0 22.4 %copy-start.4 = (f32[1536]{0:T(1024)S(1)}, f32[1536]{0:T(1024)}, u32[]{:S(2)}) copy-start(f32[1536]{0:T(1024)} %param.14) | copy-start | bytes 18436
  39.0 29.8 %copy-start.2 = (f32[31,384]{1,0:T(8,128)S(1)}, f32[31,384]{1,0:T(8,128)}, u32[]{:S(2)}) copy-start(f32[31,384]{1,0:T(8,128)} %taps_ref.3) | copy-start | bytes 142852
  61.9 8.5 %copy-start.1 = (bf16[384,1536]{1,0:T(8,128)(2,1)S(1)}, bf16[384,1536]{1,0:T(8,128)(2,1)}, u32[]{:S(2)}) copy-start(bf16[384,1536]{1,0:T(8,128)(2,1)} %weight_ref.3) | copy-start | bytes 3538948
  61.9 8.5 %collective-permute-start.2 = (bf16[16,384]{1,0:T(8,128)(2,1)S(1)}, bf16[16,384]{1,0:T(8,128)(2,1)S(1)}, u32[]{:S(2)}, u32[]{:S(2)}) collective-permute-start(bf16[16,384]{1,0:T(8,128)(2,1)S(1)} %get-tuple-element.15), channel_id=1, source_target_pairs={{1,8},{9,16},{17,24},{25,32},{33,40},{41,48},{49,56},{57,64},{65,7... | collective-permute-start | bytes 36872 | tf_op jit(solution)/shard_map/ppermute | solution.py:32
  66.8 3.6 %collective-permute-start.3 = (bf16[16,384]{1,0:T(8,128)(2,1)S(1)}, bf16[16,384]{1,0:T(8,128)(2,1)S(1)}, u32[]{:S(2)}, u32[]{:S(2)}) collective-permute-start(bf16[16,384]{1,0:T(8,128)(2,1)S(1)} %get-tuple-element.16), channel_id=1, source_target_pairs={{0,1},{1,0},{2,3},{3,2},{4,5},{5,4},{6,7},{7,6},{8,9},{9,8},{10,11... | collective-permute-start | bytes 36872 | tf_op jit(solution)/shard_map/ppermute | solution.py:36
